TPU v7x, 256 devices: a whole 4x4x8 slice. The times are simulated.
256 devices in a mesh: band: 16 (over z, core), fft: 16 (over y, x).
Axes of the slice: x: 4, y: 4, z: 8, core: 2. Of those that a mesh axis runs over, the one named last changes fastest.
Arguments:
- wave_coeffs: bfloat16 [64, 96, 18432], P('band', 'fft'), may hold values from -128 to 128
- local_potential: float32 [192, 36864], P('fft'), may hold values from -1 to 1
- projector: bfloat16 [2048, 8, 1536], P('fft'), may hold values from -0.5 to 0.5
- slot_block: int32 [2048], P('fft'), may hold values from 0 to 287
- slot_atom: int32 [2048], P('fft'), may hold values from 0 to 999
- atom_species: int32 [1000], replicated, may hold values from 0 to 3
- proj_count: int32 [4], replicated, may hold values from 4 to 8
- projector_strength: float32 [4, 8, 8], replicated, may hold values from -3 to 3
Outputs:
- result_coeffs: bfloat16 [64, 96, 18432], P('band', 'fft')
- subspace: float32 [64, 4, 64], P('band')
All inputs are finite; a program needn't handle non-finite values.
Results may differ from a plain program's by a relative error of at most 0.015.
Values may be sent and summed in bfloat16 or wider, within the bound.
No kernel may reach another device: no remote copies, remote signals or barrier semaphores. Data moves between devices by JAX's collectives and lax.ppermute only.
A program may use at most 128 MiB of HBM per device.

v0:
```python
import math

import jax
import jax.numpy as jnp
from jax import lax
from jax.sharding import PartitionSpec as P

NG = 192
KB = 96
NPROJ = 8
NSPEC = 4
NATOM = 1000


def make_table(amount, length, scaling, direction):
    frequency = jnp.arange(amount, dtype=jnp.int32) - amount // 2
    position = jnp.arange(length, dtype=jnp.int32)
    phases = frequency[:, None] * position[None, :] % length
    radians = phases.astype(jnp.float32) * (2.0 * math.pi / length)
    cosine = jnp.cos(radians) / math.sqrt(scaling)
    sine_part = direction * jnp.sin(radians) / math.sqrt(scaling)
    return jnp.stack([jnp.stack([cosine, sine_part]), jnp.stack([-sine_part, cosine])]).astype(
        jnp.bfloat16
    )


def transform(formula, values, weights_table):
    return jnp.einsum(formula, values, weights_table, preferred_element_type=jnp.float32)


def atom_matrices(atom_species, proj_count, projector_strength):
    symmetric = 0.5 * (projector_strength + jnp.swapaxes(projector_strength, 1, 2))
    channel = jnp.arange(NPROJ, dtype=jnp.int32)
    active = (channel[None, :] < proj_count[:, None]).astype(jnp.float32)
    masked = symmetric * active[:, :, None] * active[:, None, :]
    species_hot = (atom_species[:, None] == jnp.arange(NSPEC, dtype=jnp.int32)[None, :]).astype(
        jnp.float32
    )
    return jnp.einsum("at,tpq->apq", species_hot, masked, precision=lax.Precision.HIGHEST)


def intersections(left_side, right_side):
    products = jnp.einsum(
        "jkhdm,ihcm->jkdci", right_side, left_side, preferred_element_type=jnp.float32
    )
    real_part = products[:, :, 0, 0] + products[:, :, 1, 1]
    imag_part = products[:, :, 1, 0] - products[:, :, 0, 1]
    stacked = jnp.stack([real_part, imag_part], axis=2)
    return stacked.reshape(stacked.shape[0], 4, stacked.shape[3])


def on_device(
    wave_coeffs,
    local_potential,
    projector,
    slot_block,
    slot_atom,
    atom_species,
    proj_count,
    projector_strength,
):
    bands = wave_coeffs.shape[0]
    kz_dev = wave_coeffs.shape[1]
    plane_count = local_potential.shape[0]
    inverse = make_table(KB, NG, KB, 1.0)
    forward = make_table(KB, NG, NG, -1.0)
    spectra = wave_coeffs.reshape(bands, kz_dev, 2, KB, KB)
    section_x = transform("bhcfg,cdfx->bhdxg", spectra, inverse).astype(jnp.bfloat16)
    section_y = transform("bhcxg,cdgy->bhdxy", section_x, inverse).astype(jnp.bfloat16)
    real_space = transform(
        "bhcxy,cdhz->bdxyz",
        lax.all_to_all(section_y, "fft", split_axis=3, concat_axis=1, tiled=True),
        inverse,
    ).astype(jnp.bfloat16)
    block_count = plane_count * NG // 8
    blocks = real_space.reshape(bands, 2, block_count, 8 * NG)
    block_hot = slot_block[:, None] == jnp.arange(block_count, dtype=jnp.int32)[None, :]
    atom_hot = slot_atom[:, None] == jnp.arange(NATOM, dtype=jnp.int32)[None, :]
    gathered = jnp.einsum(
        "sk,bckn->bcsn", block_hot.astype(jnp.bfloat16), blocks, preferred_element_type=jnp.float32
    ).astype(jnp.bfloat16)
    slot_terms = jnp.einsum(
        "spn,bcsn->spbc", projector, gathered, preferred_element_type=jnp.float32
    )
    partial_value = jnp.einsum(
        "sa,spbc->apbc", atom_hot.astype(jnp.float32), slot_terms, precision=lax.Precision.HIGHEST
    )
    coefficients = lax.psum(partial_value, "fft")
    atom_matrix = atom_matrices(atom_species, proj_count, projector_strength)
    weighted = jnp.einsum(
        "apq,aqbc->apbc", atom_matrix, coefficients, precision=lax.Precision.HIGHEST
    ).astype(jnp.bfloat16)
    slot_weights = jnp.einsum(
        "sa,apbc->spbc", atom_hot.astype(jnp.bfloat16), weighted, preferred_element_type=jnp.float32
    ).astype(jnp.bfloat16)
    nonlocal_part = jnp.einsum(
        "spn,spbc->bcsn", projector, slot_weights, preferred_element_type=jnp.float32
    )
    nonlocal_sum = jnp.einsum(
        "sk,bcsn->bckn",
        block_hot.astype(jnp.float32),
        nonlocal_part,
        precision=lax.Precision.HIGHEST,
    )
    potential = local_potential.reshape(block_count, 8 * NG)
    applied = (potential[None, None] * blocks.astype(jnp.float32) + nonlocal_sum).astype(
        jnp.bfloat16
    )
    applied = applied.reshape(bands, 2, plane_count, NG, NG)
    back_z = transform("bcxyz,cdhz->bdxyh", applied, forward).astype(jnp.bfloat16)
    narrowed = transform(
        "bcxyh,cdgy->bdxgh",
        lax.all_to_all(back_z, "fft", split_axis=4, concat_axis=2, tiled=True),
        forward,
    ).astype(jnp.bfloat16)
    spectrum = transform("bcxgh,cdfx->bhdfg", narrowed, forward)
    kz_index = (
        lax.axis_index("fft") * kz_dev + jnp.arange(kz_dev, dtype=jnp.int32) - KB // 2
    ).astype(jnp.float32)
    kx_signed = (jnp.arange(KB, dtype=jnp.int32) - KB // 2).astype(jnp.float32)
    energy = (
        2.0
        * (
            kz_index[:, None, None] * kz_index[:, None, None]
            + kx_signed[None, :, None] * kx_signed[None, :, None]
            + kx_signed[None, None, :] * kx_signed[None, None, :]
        )
        / (KB * KB)
    )
    result = spectrum + energy[None, :, None, :, :] * spectra.astype(jnp.float32)
    result_coeffs = result.astype(jnp.bfloat16).reshape(bands, kz_dev, 2 * KB * KB)
    own_bands = jnp.stack([wave_coeffs, result_coeffs], axis=1).reshape(
        bands, 2, kz_dev, 2, KB * KB
    )
    shard_rows = lax.all_gather(wave_coeffs, "band", axis=0, tiled=True)
    left_side = shard_rows.reshape(shard_rows.shape[0], kz_dev, 2, KB * KB)
    partial_matrix = intersections(left_side, own_bands)
    subspace = lax.psum(partial_matrix, "fft") * (1.0 / (KB * KB * KB))
    return (result_coeffs, subspace)


def solution(mesh):
    return jax.shard_map(
        on_device,
        mesh=mesh,
        in_specs=(
            P("band", "fft", None),
            P("fft", None),
            P("fft", None, None),
            P("fft"),
            P("fft"),
            P(),
            P(),
            P(),
        ),
        out_specs=(P("band", "fft", None), P("band", None, None)),
        check_vma=False,
    )
```

profile of v0, /device:TPU:160, one launch (start us, length us, event | category | flops | bytes accessed | tf_op | source)
XLA Modules:
  0.0 506.1 jit_solution(4824705694059243094)
XLA Ops:
  12.1 5.5 %fusion.8 = bf16[4,6,2,192,192]{3,4,1,0,2:T(8,128)(2,1)} fusion(bf16[1,2,96,192]{2,3,0,1:T(8,128)(2,1)S(1)} %get-tuple-element.3, bf16[1,2,96,192]{2,3,0,1:T(8,128)(2,1)S(1)} %get-tuple-element.2, bf16[4,6,2,96,96]{4,3,2,0,1:T(8,128)(2,1)} %reshape.357), kind=kOutput, calls=%fused_computation.12 | convolution fusion | flops 1022459904 | bytes 4571136 | tf_op jit(solution)/shard_map/bhcxg,cdgy->bhdxy/dot_general | solution.py:28
  17.6 9.8 %copy.77 = bf16[4,6,2,192,192]{4,0,2,1,3:T(4,128)(2,1)} copy(bf16[4,6,2,192,192]{3,4,1,0,2:T(8,128)(2,1)} %fusion.8) | data formatting | bytes 7077888 | tf_op jit(solution)/shard_map/convert_element_type | solution.py:69
  27.4 63.8 %all_to_all.36 = bf16[4,6,2,192,192]{4,0,2,1,3:T(4,128)(2,1)} all-to-all(bf16[4,6,2,192,192]{4,0,2,1,3:T(4,128)(2,1)} %copy.77), channel_id=1, replica_groups=mesh['band'=16,'fft'=16] {'fft'}, dimensions={3} | all-to-all | bytes 7077888 | tf_op jit(solution)/shard_map/all_to_all | solution.py:72
  91.2 9.4 %copy.78 = bf16[4,6,2,192,192]{4,2,3,1,0:T(2,128)(2,1)} copy(bf16[4,6,2,192,192]{4,0,2,1,3:T(4,128)(2,1)} %all_to_all.36) | data formatting | bytes 7077888 | tf_op jit(solution)/shard_map/all_to_all | solution.py:72
  100.6 8.2 %copy.79 = bf16[4,16,6,2,12,192]{5,3,4,2,1,0:T(2,128)(2,1)} copy(bf16[4,16,6,2,12,192]{5,3,4,1,2,0:T(2,128)(2,1)} %bitcast.209) | data formatting | bytes 7077888 | tf_op jit(solution)/shard_map/all_to_all | solution.py:72
  108.8 7.7 %fusion.3 = bf16[4,2,12,192,192]{3,4,2,0,1:T(8,128)(2,1)} fusion(bf16[4,96,2,12,192]{4,2,3,1,0:T(2,128)(2,1)} %bitcast.208, bf16[1,2,96,192]{2,3,0,1:T(8,128)(2,1)S(1)} %get-tuple-element.3, bf16[1,2,96,192]{2,3,0,1:T(8,128)(2,1)S(1)} %get-tuple-element.2), kind=kOutput, calls=%fused_computation.5 | convolution fusion | flops 1362788352 | bytes 10764288 | tf_op jit(solution)/shard_map/bhcxy,cdhz->bdxyz/dot_general | solution.py:28
  116.5 13.0 %copy.81 = bf16[4,2,12,192,192]{4,3,2,1,0:T(8,128)(2,1)} copy(bf16[4,2,12,192,192]{3,4,2,0,1:T(8,128)(2,1)} %fusion.3) | data formatting | bytes 14155776 | tf_op jit(solution)/shard_map/convert_element_type | solution.py:74
  129.5 15.6 %reshape.358 = bf16[4,2,288,1536]{3,2,1,0:T(8,128)(2,1)} reshape(bf16[4,2,12,192,192]{4,3,2,1,0:T(8,128)(2,1)} %copy.81) | data formatting | bytes 14155776 | tf_op jit(solution)/shard_map/reshape | solution.py:76
  145.0 7.4 %fusion.15 = bf16[4,2,128,1536]{2,3,1,0:T(8,128)(2,1)} fusion(bf16[4,2,288,1536]{3,2,1,0:T(8,128)(2,1)} %reshape.358, s32[128]{0:T(128)S(1)} %copy-done.10), kind=kOutput, calls=%fused_computation.23 | convolution fusion | flops 907579392 | bytes 10224128 | tf_op jit(solution)/shard_map/sk,bckn->bcsn/dot_general | solution.py:79
  152.4 6.2 %copy.84 = bf16[4,2,128,1536]{3,0,1,2:T(4,128)(2,1)} copy(bf16[4,2,128,1536]{2,3,1,0:T(8,128)(2,1)} %fusion.15) | data formatting | bytes 6291456 | tf_op jit(solution)/shard_map/convert_element_type | solution.py:81
  172.9 82.3 %all-reduce.2.cloned.1.call-done = f32[1000,8,4,2]{0,1,3,2:T(8,128)} async-done(((f32[1000,8,4,2]{0,1,3,2:T(8,128)}), f32[1000,8,4,2]{0,1,3,2:T(8,128)}) %all-reduce.2.cloned.1.call-update) | async-done | bytes 256016 | tf_op jit(solution)/shard_map/psum | solution.py:88
  259.5 11.0 %convolution_convert_fusion.1 = bf16[1000,8,4,2]{1,2,3,0:T(4,128)(2,1)S(1)} fusion(f32[1000,8,8,1]{2,1,3,0:T(8,128)} %copy.120, f32[1000,8,4,2]{1,2,3,0:T(4,128)} %copy.87), kind=kOutput, calls=%fused_computation.35 | convolution fusion | flops 6208000 | bytes 640000 | tf_op jit(solution)/shard_map/apq,aqbc->apbc/dot_general | solution.py:90
  272.9 14.0 %fusion.2 = bf16[4,2,288,1536]{3,2,1,0:T(8,128)(2,1)} fusion(bf16[4,2,288,1536]{3,2,1,0:T(8,128)(2,1)} %reshape.358, f32[288,1536]{1,0:T(8,128)S(1)} %copy-done.2, f32[4,2,128,1536]{3,0,1,2:T(4,128)S(1)} %convolution_bitcast_fusion, s32[128]{0:T(128)S(1)} %copy-done.11), kind=kOutput, calls=%fused_computation.4 | convolution fusion | flops 5450010624 | bytes 22217216 | tf_op jit(solution)/shard_map/sk,bcsn->bckn/dot_general | solution.py:99
  286.9 15.0 %reshape.359 = bf16[4,2,12,192,192]{4,3,2,1,0:T(8,128)(2,1)} reshape(bf16[4,2,288,1536]{3,2,1,0:T(8,128)(2,1)} %fusion.2) | data formatting | bytes 14155776 | tf_op jit(solution)/shard_map/reshape | solution.py:109
  301.9 6.8 %fusion.9 = bf16[4,2,12,192,96]{3,4,2,0,1:T(8,128)(2,1)S(1)} fusion(bf16[4,2,12,192,192]{4,3,2,1,0:T(8,128)(2,1)} %reshape.359, bf16[1,2,96,192]{2,3,1,0:T(8,128)(2,1)S(1)} %copy-done.5, bf16[1,2,96,192]{2,3,1,0:T(8,128)(2,1)S(1)} %get-tuple-element.4), kind=kOutput, calls=%fused_computation.13 | convolution fusion | flops 1360797696 | bytes 10764288 | tf_op jit(solution)/shard_map/bcxyz,cdhz->bdxyh/dot_general | solution.py:28
  308.7 5.9 %copy.93 = bf16[4,2,12,192,96]{3,0,2,1,4:T(4,128)(2,1)} copy(bf16[4,2,12,192,96]{3,4,2,0,1:T(8,128)(2,1)S(1)} %fusion.9) | data formatting | bytes 7077888 | tf_op jit(solution)/shard_map/convert_element_type | solution.py:110
  314.6 5.3 %all-to-all-start.1 = ((bf16[4,2,12,192,96]{3,0,2,1,4:T(4,128)(2,1)}), bf16[4,2,12,192,96]{3,0,2,1,4:T(4,128)(2,1)}, u32[]{:S(2)}, u32[]{:S(2)}) async-start(bf16[4,2,12,192,96]{3,0,2,1,4:T(4,128)(2,1)} %copy.93), calls=%async_computation.1 | async-start | bytes 9437184 | tf_op jit(solution)/shard_map/all_to_all | solution.py:113
  322.0 65.2 %all-to-all-done.1 = bf16[4,2,12,192,96]{3,0,2,1,4:T(4,128)(2,1)} async-done(((bf16[4,2,12,192,96]{3,0,2,1,4:T(4,128)(2,1)}), bf16[4,2,12,192,96]{3,0,2,1,4:T(4,128)(2,1)}, u32[]{:S(2)}, u32[]{:S(2)}) %all-to-all-start.1) | async-done | bytes 3538976 | tf_op jit(solution)/shard_map/all_to_all | solution.py:113
  387.2 9.7 %copy.94 = bf16[4,2,12,192,96]{3,1,4,2,0:T(2,128)(2,1)} copy(bf16[4,2,12,192,96]{3,0,2,1,4:T(4,128)(2,1)} %all-to-all-done.1) | data formatting | bytes 7077888 | tf_op jit(solution)/shard_map/all_to_all | solution.py:113
  396.9 8.2 %copy.95 = bf16[4,2,16,12,192,6]{4,1,5,3,2,0:T(2,128)(2,1)} copy(bf16[4,2,16,12,192,6]{4,1,5,2,3,0:T(2,128)(2,1)} %bitcast.210) | data formatting | bytes 7077888 | tf_op jit(solution)/shard_map/all_to_all | solution.py:113
  405.1 5.2 %fusion.26 = bf16[4,6,2,96,96]{4,3,1,0,2:T(8,128)(2,1)S(1)} fusion(bf16[2,2,96,192,1,1]{2,3,1,0,5,4:T(8,128)(2,1)S(1)} %maximum_bitcast_fusion.4, bf16[4,2,192,192,6,1]{3,1,4,2,0,5:T(2,128)(2,1)} %bitcast.212, bf16[4,6,2,96,96]{4,3,2,0,1:T(8,128)(2,1)S(1)} %copy-done.4, f32[6,96,96]{2,1,0:T(8,128)S(1)} %add_multiply_fusion), kind=kOutput, calls=%fused_computation.31 | convolution fusion | flops 1021870080 | bytes 5677056 | tf_op jit(solution)/shard_map/bcxgh,cdfx->bhdfg/dot_general | solution.py:28
  418.6 30.6 %reshape.388 = bf16[64,6,2,9216]{3,2,1,0:T(2,128)(2,1)} reshape(bf16[64,6,18432]{2,1,0:T(8,128)(2,1)} %all-gather.2.cloned.1.call-done) | data formatting | bytes 28311552 | tf_op jit(solution)/shard_map/reshape | solution.py:136
  449.2 11.8 %fusion.49 = f32[4,2,2,2,64]{4,0,3,2,1:T(4,128)S(1)} fusion(bf16[64,6,2,9216,1,1]{3,2,1,0,5,4:T(2,128)(2,1)} %bitcast.211, bf16[4,1,6,2,9216]{4,0,2,3,1:T(4,128)(2,1)} %copy.104, bf16[4,1,6,2,9216]{4,0,2,3,1:T(4,128)(2,1)} %copy.103), kind=kOutput, calls=%fused_computation.43 | convolution fusion | flops 230031360 | bytes 15933440 | tf_op jit(solution)/shard_map/jkhdm,ihcm->jkdci/dot_general | solution.py:43
  461.1 36.5 %psum.15 = f32[4,4,64]{2,1,0:T(4,128)S(1)} all-reduce(f32[4,4,64]{2,1,0:T(4,128)S(1)} %bitcast.213), channel_id=1, replica_groups=mesh['band'=16,'fft'=16] {'fft'}, use_global_device_ids=true, to_apply=%region_1.2 | all-reduce | flops 1024 | bytes 8192 | tf_op jit(solution)/shard_map/psum | solution.py:138
  (70 shorter events, 36.0 us)
Async XLA Ops:
  8.0 150.7 %copy-start = (bf16[128,8,1536]{2,1,0:T(8,128)(2,1)S(1)}, bf16[128,8,1536]{2,1,0:T(8,128)(2,1)}, u32[]{:S(2)}) copy-start(bf16[128,8,1536]{2,1,0:T(8,128)(2,1)} %param.10) | copy-start | bytes 9437188
  8.0 247.2 %all-reduce.2.cloned.1.call-start = ((), (), s32[]{:S(2)}) async-start(), calls=%async_computation.2 | async-start | bytes 524288 | tf_op jit(solution)/shard_map/psum | solution.py:88
  129.5 15.6 %copy-start.10 = (s32[128]{0:T(128)S(1)}, s32[128]{0:T(128)}, u32[]{:S(2)}) copy-start(s32[128]{0:T(128)} %param.11) | copy-start | bytes 1540
  158.7 3.4 copy-start.13
  162.1 4.2 copy-start.8
  162.1 4.3 copy-start.12
  162.1 4.5 copy-start.9
  163.5 255.1 %all-gather.2.cloned.1.call-start = ((), (), s32[]{:S(2)}) async-start(), calls=%async_computation.3 | async-start | bytes 20054016 | tf_op jit(solution)/shard_map/all_gather | solution.py:135
  169.4 2.8 copy-start.6
  169.4 2.8 copy-start.7
  259.5 11.0 %copy-start.14 = (s32[128]{0:T(128)S(1)}, s32[128]{0:T(128)}, u32[]{:S(2)}) copy-start(s32[128]{0:T(128)} %param.12) | copy-start | bytes 1540
  271.5 1.5 copy-start.2
  271.5 1.5 copy-start.11
  286.9 15.0 %copy-start.5 = (bf16[1,2,96,192]{2,3,1,0:T(8,128)(2,1)S(1)}, bf16[1,2,96,192]{2,3,1,0:T(8,128)(2,1)}, u32[]{:S(2)}) copy-start(bf16[1,2,96,192]{2,3,1,0:T(8,128)(2,1)} %get-tuple-element.5) | copy-start | bytes 221188
  314.6 5.3 %copy-start.3 = (bf16[4,6,18432]{2,0,1:T(4,128)(2,1)S(1)}, bf16[4,6,18432]{2,0,1:T(4,128)(2,1)}, u32[]{:S(2)}) copy-start(bf16[4,6,18432]{2,0,1:T(4,128)(2,1)} %param.8) | copy-start | bytes 2654212
  314.6 72.6 %all-to-all-start.1 = ((bf16[4,2,12,192,96]{3,0,2,1,4:T(4,128)(2,1)}), bf16[4,2,12,192,96]{3,0,2,1,4:T(4,128)(2,1)}, u32[]{:S(2)}, u32[]{:S(2)}) async-start(bf16[4,2,12,192,96]{3,0,2,1,4:T(4,128)(2,1)} %copy.93), calls=%async_computation.1 | async-start | bytes 9437184 | tf_op jit(solution)/shard_map/all_to_all | solution.py:113
  396.9 8.2 %copy-start.4 = (bf16[4,6,2,96,96]{4,3,2,0,1:T(8,128)(2,1)S(1)}, bf16[4,6,2,96,96]{4,3,2,0,1:T(8,128)(2,1)}, u32[]{:S(2)}) copy-start(bf16[4,6,2,96,96]{4,3,2,0,1:T(8,128)(2,1)} %reshape.357) | copy-start | bytes 2654212
  449.2 49.0 %copy-start.1 = (bf16[128,8,1536]{2,1,0:T(8,128)(2,1)S(1)}, bf16[128,8,1536]{2,1,0:T(8,128)(2,1)}, u32[]{:S(2)}) copy-start(bf16[128,8,1536]{2,1,0:T(8,128)(2,1)} %param.10) | copy-start | bytes 9437188
Sparse Core Ops, SparseCore 0:
  163.6 91.5 all-reduce.1
Sparse Core Ops, SparseCore 1:
  166.3 100.5 all-gather.1
where the time goes:
time: 514 us; the launch traced here: 506 us
  local copies, waits for them, and re-layouts  158 us (31%)
  waiting for transfers between devices  148 us (29%)
  blocking collectives  100 us (19%)
  matrix products  76.1 us (15%)
  between operations  16.2 us (3%)
  starting transfers between devices  5.38 us (1%)
    psum x1, waiting for transfers between devices, on_device(): coefficients = lax.psum(partial_value, 'fft')  82.3 us
    all_to_all x1, waiting for transfers between devices, on_device(): lax.all_to_all(back_z, 'fft', split_axis=4, concat_axis=2, tiled=True)  65.2 us
    all_to_all x1, blocking collectives, on_device(): lax.all_to_all(section_y, 'fft', split_axis=3, concat_axis=1, tiled=True)  63.8 us
    psum x1, blocking collectives, on_device(): subspace = lax.psum(partial_matrix, 'fft') * (1.0 / (KB * KB * KB))  36.5 us
    reshape x1, local copies, waits for them, and re-layouts, on_device(): left_side = shard_rows.reshape(shard_rows.shape[0], kz_dev, 2, KB * KB)  30.6 us
    dot_general x4, matrix products, transform(): jnp.einsum(formula, values, weights_table, preferred_element_type=jnp.flo...  25.2 us
    all_to_all x2, local copies, waits for them, and re-layouts, on_device(): lax.all_to_all(back_z, 'fft', split_axis=4, concat_axis=2, tiled=True)  17.9 us
    all_to_all x2, local copies, waits for them, and re-layouts, on_device(): lax.all_to_all(section_y, 'fft', split_axis=3, concat_axis=1, tiled=True)  17.6 us
  transfers between devices with their start and end apart: 3, of which 2 were waited for; matrix products, arithmetic and copies ran while one was open for 20% of the time, Pallas kernels for 0%

commit v1 on v0

v1 whole, which is shorter than its diff:
```python
import math

import jax
import jax.numpy as jnp
import ml_dtypes
import numpy as np
from jax import lax
from jax.experimental import pallas as pl
from jax.experimental.pallas import tpu as pltpu
from jax.sharding import PartitionSpec as P

NG = 192
KB = 96
NPROJ = 8
NSPEC = 4
ND = 16
XD = NG // ND
HD = KB // ND
NBD = 4
SD = 128
NBLK = XD * NG // 8
DX = 2 * XD
LANES = HD * NBD * KB
TILES = LANES // 128
GROUP = NBD * KB
PLANE = 2 * KB * KB
BF = jnp.bfloat16
F32 = jnp.float32
HIGH = lax.Precision.HIGHEST
MIB = 1024 * 1024
PLANE_UNROLL = 2


def table(scaling, direction):
    phases = ((np.arange(KB) - KB // 2)[:, None] * np.arange(NG)[None, :]) % NG
    radians = phases.astype(np.float64) * (2.0 * math.pi / NG)
    cosine = np.cos(radians) / math.sqrt(scaling)
    sine = direction * np.sin(radians) / math.sqrt(scaling)
    full = np.stack([np.stack([cosine, sine]), np.stack([-sine, cosine])])
    return full.astype(np.float32).astype(ml_dtypes.bfloat16)


def pad_last(array, width):
    return np.pad(array, [(0, 0)] * (array.ndim - 1) + [(0, width - array.shape[-1])])


def constants():
    inverse = table(KB, 1.0)
    forward = table(NG, -1.0)
    out = {}
    inv_x = inverse.reshape(2, 2, KB, ND, XD)
    out["a"] = inv_x.transpose(3, 1, 4, 0, 2).reshape(ND * DX, 2 * KB)
    real_part = pad_last(inverse[0, 0].T, 128)
    imag_part = pad_last(inverse[0, 1].T, 128)
    out["by"] = np.concatenate([real_part, imag_part], axis=1)
    inv_z = inverse.reshape(2, 2, ND, HD, NG).transpose(0, 3, 2, 1, 4)
    out["bz"] = pad_last(inv_z, 256).reshape(2 * KB, 512)
    fwd_z = forward.reshape(2, 2, ND, HD, NG).transpose(1, 3, 2, 0, 4)
    out["cz"] = pad_last(fwd_z, 256).reshape(2 * KB, 512)
    out["cy"] = pad_last(forward.transpose(0, 3, 1, 2), 128).reshape(2, NG, 256)
    fwd_x = forward.reshape(2, 2, KB, ND, XD)
    out["d"] = fwd_x.transpose(1, 2, 3, 0, 4).reshape(2 * KB, ND * DX)
    return out


def dot(left, right):
    return jnp.dot(left, right, preferred_element_type=F32)


def dot_nt(left, right):
    return lax.dot_general(left, right, (((1,), (1,)), ((), ())), preferred_element_type=F32)


def iota(shape, axis):
    return lax.broadcasted_iota(jnp.int32, shape, axis)


def x_kernel(table_ref, wave_ref, out_ref):
    for h in range(HD):
        parts = [
            jnp.concatenate([wave_ref[h, b].astype(F32), jnp.zeros((2 * KB, 32), F32)], axis=1)
            for b in range(NBD)
        ]
        right = jnp.concatenate(join_bands(parts), axis=1).astype(BF)
        out_ref[:, h * GROUP : (h + 1) * GROUP] = dot(table_ref[...], right).astype(BF)


def x_transform(table_x, wave):
    return pl.pallas_call(
        x_kernel,
        out_shape=jax.ShapeDtypeStruct((ND * DX, LANES), BF),
        compiler_params=pltpu.CompilerParams(vmem_limit_bytes=60 * MIB),
        name="x_transform",
    )(table_x, wave)


def split_bands(first, second, third):
    lane = iota(first.shape, 1)
    one = pltpu.roll(jnp.where(lane >= 96, first, second), 32, 1)
    two = pltpu.roll(jnp.where(lane >= 64, second, third), 64, 1)
    return first, one, two, pltpu.roll(third, 96, 1)


def join_bands(parts):
    lane = iota(parts[0].shape, 1)
    one = pltpu.roll(parts[1], 96, 1)
    two = pltpu.roll(parts[2], 64, 1)
    three = pltpu.roll(parts[3], 32, 1)
    return (
        jnp.where(lane < 96, parts[0], one),
        jnp.where(lane < 64, one, two),
        jnp.where(lane < 32, two, three),
    )


def grid_kernel(
    slot_ref, ty_ref, tz_ref, fold_ref, sums_ref, ids_ref, in_ref, proj_in_ref,
    exch_ref, real_ref,
    held_ref, proj_ref, wide_ref, space_ref, terms_ref, in_sems, proj_sem, out_sems,
):
    def columns_in(h):
        columns = pl.ds(h * GROUP, GROUP)
        return pltpu.make_async_copy(in_ref.at[:, columns], held_ref.at[h], in_sems.at[h])

    def plane_out(plane):
        blocks = pl.ds(plane * (NG // 8), NG // 8)
        return pltpu.make_async_copy(space_ref.at[blocks], real_ref.at[blocks], out_sems.at[plane])

    for h in range(HD):
        columns_in(h).start()
    projector_in = pltpu.make_async_copy(proj_in_ref, proj_ref, proj_sem)
    projector_in.start()
    for h in range(HD):
        columns_in(h).wait()
        for v in range(3):
            wide_ref[3 * h + v] = held_ref[h, :, v * 128 : v * 128 + 128].astype(F32)

    def plane_step(plane, carry):
        pieces = []
        for d in range(2):
            rows = pl.ds(d * XD + plane, ND, stride=DX)
            columns = [
                jnp.concatenate([wide_ref[3 * h + v, rows, :] for h in range(HD)], axis=0)
                for v in range(3)
            ]
            pieces.append(split_bands(*columns))
        section = []
        for b in range(NBD):
            real_part, imag_part = pieces[0][b], pieces[1][b]
            right = jnp.concatenate(
                [
                    jnp.concatenate([real_part, -imag_part], axis=1),
                    jnp.concatenate([imag_part, real_part], axis=1),
                ],
                axis=0,
            ).astype(BF)
            section.append(dot_nt(ty_ref[...], right).astype(BF))
        whole = dot(jnp.concatenate(section, axis=0), tz_ref[...])
        for b in range(NBD):
            cells = whole[NG * b : NG * b + NG]
            both = jnp.concatenate(
                [cells[:, :256].reshape(NG // 8, 8, 256), cells[:, 256:].reshape(NG // 8, 8, 256)],
                axis=1,
            ).astype(BF)
            space_ref[pl.ds(plane * (NG // 8), NG // 8), 16 * b : 16 * b + 16, :] = both
        plane_out(plane).start()
        return carry

    lax.fori_loop(0, XD, plane_step, 0, unroll=PLANE_UNROLL)
    projector_in.wait()
    lane = iota((8, 64), 1) % 8

    def slot(s, carry):
        cells = space_ref[slot_ref[s]]
        product = dot_nt(proj_ref[s], cells[:, :NG]).reshape(8, 8, 64)
        total = jnp.where(lane == 0, product[0], 0.0)
        for y in range(1, 8):
            total = jnp.where(lane == y, product[y], total)
        terms_ref[pl.ds(pl.multiple_of(s * 8, 8), 8), :] = total
        return carry

    lax.fori_loop(0, SD, slot, 0, unroll=8)
    terms = terms_ref[...]
    high = terms.astype(BF)
    low = (terms - high.astype(F32)).astype(BF)
    folded = dot(high, fold_ref[...]) + dot(low, fold_ref[...])
    keep = iota(folded.shape, 0) % 8 == iota(folded.shape, 1) % 64 // 8
    folded = jnp.where(keep, folded, 0.0).astype(BF)
    ordered = dot(sums_ref[...], folded)
    packed = jnp.where(iota((64, 128), 1) < 64, ordered[:64], ordered[64:]).astype(BF)
    for k in range(ND):
        exch_ref[k, 0:64, :] = packed
        exch_ref[k, 64:80, :] = ids_ref[...]
    for plane in range(XD):
        plane_out(plane).wait()


def grid_part(tables, received, projector, slot_block, ids):
    fold = np.zeros((64, 128), np.float32)
    for bc in range(8):
        for y in range(8):
            fold[bc * 8 + y, bc::8] = 1.0
    sums = (np.arange(1024)[None, :] // 8 == np.arange(128)[:, None]).astype(np.float32)
    vmem, anywhere = pl.BlockSpec(memory_space=pltpu.VMEM), pl.BlockSpec(memory_space=pl.ANY)
    return pl.pallas_call(
        grid_kernel,
        in_specs=[pl.BlockSpec(memory_space=pltpu.SMEM)] + [vmem] * 5 + [anywhere] * 2,
        out_specs=[vmem, anywhere],
        out_shape=[
            jax.ShapeDtypeStruct((ND, 80, 128), BF),
            jax.ShapeDtypeStruct((NBLK, 64, 256), BF),
        ],
        scratch_shapes=[
            pltpu.VMEM((HD, ND * DX, GROUP), BF),
            pltpu.VMEM((SD, 64, NG), BF),
            pltpu.VMEM((TILES, ND * DX, 128), F32),
            pltpu.VMEM((NBLK, 64, 256), BF),
            pltpu.VMEM((SD * 8, 64), F32),
            pltpu.SemaphoreType.DMA((HD,)),
            pltpu.SemaphoreType.DMA,
            pltpu.SemaphoreType.DMA((XD,)),
        ],
        compiler_params=pltpu.CompilerParams(vmem_limit_bytes=60 * MIB),
        name="grid_part",
    )(
        slot_block, tables["by"], tables["bz"], jnp.asarray(fold, BF), jnp.asarray(sums, BF), ids,
        received, projector,
    )


def apply_kernel(
    slot_ref, exch_ref, own_ref, kinds_ref, mix_ref, rep_ref, spread_ref, tz_ref, ty_ref,
    real_in_ref, pot_in_ref, proj_in_ref,
    out_ref,
    real_ref, pot_ref, proj_ref, field_ref, wide_ref, weight_ref, real_sems, pot_sems, proj_sem,
):
    def plane_in(plane):
        blocks = pl.ds(plane * (NG // 8), NG // 8)
        return (
            pltpu.make_async_copy(real_in_ref.at[blocks], real_ref.at[blocks], real_sems.at[plane]),
            pltpu.make_async_copy(pot_in_ref.at[blocks], pot_ref.at[blocks], pot_sems.at[plane]),
        )

    for plane in range(XD):
        for copy in plane_in(plane):
            copy.start()
    projector_in = pltpu.make_async_copy(proj_in_ref, proj_ref, proj_sem)
    projector_in.start()

    row, col = iota((128, 128), 0), iota((128, 128), 1)
    halves = (row < 64) == (col < 64)
    total = jnp.zeros((SD, 128), F32)
    for source in range(ND):
        ids = exch_ref[source, 64:80, :].astype(F32)
        atoms = ids[0:1] * 32.0 + ids[1:2]
        same = jnp.where(own_ref[...] == atoms, 1.0, 0.0).astype(BF)
        terms = exch_ref[source, 0:64, :].astype(F32)
        terms = jnp.where(halves, jnp.concatenate([terms, terms], axis=0), 0.0).astype(BF)
        total = total + dot(same, terms)
    total = total + pltpu.roll(total, 64, 1)
    mixed = jnp.dot(total, mix_ref[...], preferred_element_type=F32, precision=HIGH)
    mixed = mixed * kinds_ref[...]
    mixed = mixed[:, :128] + mixed[:, 128:]
    weighted = (mixed + pltpu.roll(mixed, 64, 1)).astype(BF)
    spread = dot(rep_ref[...], weighted)
    keep = iota(spread.shape, 0) % 8 == iota(spread.shape, 1) % 8
    spread = jnp.where(keep, spread, 0.0).astype(BF)
    weight_ref[...] = dot(spread, spread_ref[...])

    def potential_step(plane, carry):
        for copy in plane_in(plane):
            copy.wait()
        for yb in range(NG // 8):
            block = plane * (NG // 8) + yb
            cells = real_ref[block].astype(F32).reshape(8, 8, 256)
            values = pot_ref[block]
            values = jnp.concatenate([values, jnp.zeros((8, 64), F32)], axis=1)
            field_ref[block] = (cells * values[None]).reshape(64, 256)
        return carry

    lax.fori_loop(0, XD, potential_step, 0)
    projector_in.wait()
    own = (iota((8, 64), 1) // 8 == iota((8, 64), 0)).astype(F32)

    def slot(s, carry):
        rows = weight_ref[pl.ds(pl.multiple_of(s * 8, 8), 8), :]
        matrix = (rows[:, None, :] * own[None]).reshape(64, 64).astype(BF)
        block = slot_ref[s]
        field_ref[block, :, :NG] = field_ref[block, :, :NG] + dot(matrix, proj_ref[s])
        return carry

    lax.fori_loop(0, SD, slot, 0, unroll=8)

    def plane_step(plane, carry):
        start = plane * (NG // 8)
        parts = []
        for b in range(NBD):
            zero = field_ref[pl.ds(start, NG // 8), 16 * b : 16 * b + 8, :].reshape(NG, 256)
            one = field_ref[pl.ds(start, NG // 8), 16 * b + 8 : 16 * b + 16, :].reshape(NG, 256)
            cells = jnp.concatenate([zero, one], axis=1).astype(BF)
            parts.append(dot_nt(tz_ref[...], cells).astype(BF))
        both = dot(jnp.concatenate([part[:KB] for part in parts], axis=0), ty_ref[0])
        both = both + dot(jnp.concatenate([part[KB:] for part in parts], axis=0), ty_ref[1])
        for d in range(2):
            joined = join_bands(
                [both[KB * b : KB * b + KB, 128 * d : 128 * d + 128] for b in range(NBD)]
            )
            rows = pl.ds(d * XD + plane, ND, stride=DX)
            for h in range(HD):
                for v in range(3):
                    wide_ref[3 * h + v, rows, :] = joined[v][16 * h : 16 * h + 16]
        return carry

    lax.fori_loop(0, XD, plane_step, 0, unroll=PLANE_UNROLL)
    for t in range(TILES):
        out_ref[:, t * 128 : t * 128 + 128] = wide_ref[t].astype(BF)


def apply_part(tables, exchanged, own, kinds, mix, real_space, potential, projector, slot_block):
    rep = (np.arange(1024)[:, None] // 8 == np.arange(128)[None, :]).astype(np.float32)
    spread = np.zeros((128, 64), np.float32)
    for p in range(8):
        spread[p * 8 : p * 8 + 8, p::8] = 1.0
    vmem, anywhere = pl.BlockSpec(memory_space=pltpu.VMEM), pl.BlockSpec(memory_space=pl.ANY)
    return pl.pallas_call(
        apply_kernel,
        in_specs=[pl.BlockSpec(memory_space=pltpu.SMEM)] + [vmem] * 8 + [anywhere] * 3,
        out_specs=vmem,
        out_shape=jax.ShapeDtypeStruct((ND * DX, LANES), BF),
        scratch_shapes=[
            pltpu.VMEM((NBLK, 64, 256), BF),
            pltpu.VMEM((NBLK, 8, NG), F32),
            pltpu.VMEM((SD, 64, NG), BF),
            pltpu.VMEM((NBLK, 64, 256), F32),
            pltpu.VMEM((TILES, ND * DX, 128), F32),
            pltpu.VMEM((SD * 8, 64), F32),
            pltpu.SemaphoreType.DMA((XD,)),
            pltpu.SemaphoreType.DMA((XD,)),
            pltpu.SemaphoreType.DMA,
        ],
        compiler_params=pltpu.CompilerParams(vmem_limit_bytes=60 * MIB),
        name="apply_part",
    )(
        slot_block, exchanged, own, kinds, mix, jnp.asarray(rep, BF), jnp.asarray(spread, BF),
        tables["cz"], tables["cy"], real_space, potential, projector,
    )


def back_kernel(kz_ref, table_ref, in_ref, wave_ref, squares_ref, out_ref):
    for h in range(HD):
        kz = (kz_ref[0] + (h - KB // 2)).astype(F32)
        energy = (squares_ref[...] + kz * kz) * (2.0 / (KB * KB))
        spectrum = dot(table_ref[...], in_ref[:, h * GROUP : (h + 1) * GROUP])
        parts = split_bands(spectrum[:, :128], spectrum[:, 128:256], spectrum[:, 256:])
        for b in range(NBD):
            own = wave_ref[h, b].astype(F32)
            out_ref[h, b] = (parts[b][:, :KB] + energy * own).astype(BF)


def back_transform(table_x, first_kz, received, wave):
    signed = np.arange(KB) - KB // 2
    squares = (signed * signed)[:, None] + (signed * signed)[None, :]
    squares = np.tile(squares, (2, 1)).astype(np.float32)
    return pl.pallas_call(
        back_kernel,
        in_specs=[pl.BlockSpec(memory_space=pltpu.SMEM)]
        + [pl.BlockSpec(memory_space=pltpu.VMEM)] * 4,
        out_shape=jax.ShapeDtypeStruct((HD, NBD, 2 * KB, KB), BF),
        compiler_params=pltpu.CompilerParams(vmem_limit_bytes=60 * MIB),
        name="back_transform",
    )(first_kz, table_x, received, wave, jnp.asarray(squares))


ROWS = HD * NBD
CHUNK = 2304
CHUNKS = KB * KB // CHUNK


def subspace_kernel(
    all0_ref, all1_ref, wave0_ref, wave1_ref, result0_ref, result1_ref,
    fold0_ref, fold1_ref, rows_ref,
    out_ref,
    acc0, acc1,
):
    step = pl.program_id(0)

    @pl.when(step == 0)
    def _():
        acc0[...] = jnp.zeros_like(acc0)
        acc1[...] = jnp.zeros_like(acc1)

    own = [wave0_ref, result0_ref, wave1_ref, result1_ref]
    right = jnp.concatenate([ref[...].astype(F32) for ref in own], axis=0).astype(BF)
    acc0[...] += dot_nt(all0_ref[...], right)
    acc1[...] += dot_nt(all1_ref[...], right)

    @pl.when(step == CHUNKS - 1)
    def _():
        shape = acc0.shape
        keep = iota(shape, 0) % ROWS // NBD == iota(shape, 1) % ROWS // NBD
        folded = jnp.dot(
            jnp.where(keep, acc0[...], 0.0), fold0_ref[...], precision=HIGH
        ) + jnp.dot(jnp.where(keep, acc1[...], 0.0), fold1_ref[...], precision=HIGH)
        turned = jnp.dot(folded.T[:16], rows_ref[...], precision=HIGH)
        packed = jnp.where(iota((8, 128), 1) < 64, turned[:8], turned[8:])
        for k in range(ND):
            out_ref[k] = packed


def subspace_part(everything, wave, result):
    fold0 = np.zeros((2, 2, HD, NBD, 128), np.float32)
    fold1 = np.zeros((2, 2, HD, NBD, 128), np.float32)
    for k in range(2):
        for j in range(NBD):
            fold0[0, k, :, j, 4 * j + 2 * k] = 1.0
            fold0[1, k, :, j, 4 * j + 2 * k + 1] = 1.0
            fold1[1, k, :, j, 4 * j + 2 * k] = 1.0
            fold1[0, k, :, j, 4 * j + 2 * k + 1] = -1.0
    total = everything.shape[0]
    row = np.arange(total)
    band = row // ROWS * NBD + row % NBD
    rows = (band[:, None] == np.arange(128)[None, :] % 64).astype(np.float32)
    whole = lambda *shape: pl.BlockSpec(shape, lambda i: (0,) * len(shape))
    return pl.pallas_call(
        subspace_kernel,
        grid=(CHUNKS,),
        in_specs=[
            pl.BlockSpec((total, CHUNK), lambda i: (0, i)),
            pl.BlockSpec((total, CHUNK), lambda i: (0, CHUNKS + i)),
            pl.BlockSpec((ROWS, CHUNK), lambda i: (0, i)),
            pl.BlockSpec((ROWS, CHUNK), lambda i: (0, CHUNKS + i)),
            pl.BlockSpec((ROWS, CHUNK), lambda i: (0, i)),
            pl.BlockSpec((ROWS, CHUNK), lambda i: (0, CHUNKS + i)),
            whole(4 * ROWS, 128),
            whole(4 * ROWS, 128),
            whole(total, 128),
        ],
        out_specs=whole(ND, 8, 128),
        out_shape=jax.ShapeDtypeStruct((ND, 8, 128), F32),
        scratch_shapes=[pltpu.VMEM((total, 4 * ROWS), F32), pltpu.VMEM((total, 4 * ROWS), F32)],
        compiler_params=pltpu.CompilerParams(vmem_limit_bytes=60 * MIB),
        name="subspace_part",
    )(
        everything, everything, wave, wave, result, result,
        jnp.asarray(fold0.reshape(-1, 128)), jnp.asarray(fold1.reshape(-1, 128)), jnp.asarray(rows),
    )


def exchange(array):
    return lax.all_to_all(array, "fft", split_axis=0, concat_axis=0, tiled=True)


def on_device(
    wave_coeffs,
    local_potential,
    projector,
    slot_block,
    slot_atom,
    atom_species,
    proj_count,
    projector_strength,
):
    tables = {name: jnp.asarray(value) for name, value in constants().items()}
    rows = wave_coeffs.transpose(1, 0, 2)
    wave = rows.reshape(HD, NBD, 2 * KB, KB)
    projector = projector.reshape(SD, NPROJ, 8, NG).transpose(0, 2, 1, 3).reshape(SD, 64, NG)
    potential = local_potential.reshape(NBLK, 8, NG)
    ids = jnp.concatenate(
        [(slot_atom // 32)[None], (slot_atom % 32)[None], jnp.zeros((14, SD), jnp.int32)]
    ).astype(BF)
    own_ids = jnp.broadcast_to(slot_atom.astype(F32)[:, None], (SD, 128))
    species = jnp.take(atom_species, slot_atom, axis=0)
    kinds = (species[:, None] == jnp.arange(256, dtype=jnp.int32)[None, :] // 64).astype(F32)
    symmetric = 0.5 * (projector_strength + jnp.swapaxes(projector_strength, 1, 2))
    active = (jnp.arange(NPROJ, dtype=jnp.int32)[None, :] < proj_count[:, None]).astype(F32)
    masked = symmetric * active[:, :, None] * active[:, None, :]
    mix = masked.transpose(2, 0, 1)[:, None, :, :, None] * jnp.eye(8, dtype=F32)[None, :, None, None]
    mix = jnp.pad(mix.reshape(64, 256), ((0, 64), (0, 0)))

    sent = x_transform(tables["a"], wave)
    sent, rows = lax.optimization_barrier((sent, rows))
    flat = rows.reshape(ROWS, PLANE)
    everything = lax.all_gather(flat, "band", axis=0, tiled=True)
    received = exchange(sent.reshape(ND, DX, LANES)).reshape(ND * DX, LANES)
    terms, real_space = grid_part(tables, received, projector, slot_block, ids)
    exchanged = exchange(terms)
    sent = apply_part(
        tables, exchanged, own_ids, kinds, mix, real_space, potential, projector, slot_block
    )
    received = exchange(sent.reshape(ND, DX, LANES)).reshape(ND * DX, LANES)
    first_kz = (lax.axis_index("fft") * HD).astype(jnp.int32).reshape(1)
    result = back_transform(tables["d"], first_kz, received, wave)
    result = result.reshape(ROWS, PLANE)
    partial = subspace_part(everything, flat, result)
    summed = exchange(partial).sum(axis=0) * (1.0 / (KB * KB * KB))
    subspace = summed.reshape(8, 2, 64).transpose(1, 0, 2).reshape(NBD, 4, 64)
    result_coeffs = result.reshape(HD, NBD, PLANE).transpose(1, 0, 2)
    return (result_coeffs, subspace)


def solution(mesh):
    return jax.shard_map(
        on_device,
        mesh=mesh,
        in_specs=(
            P("band", "fft", None),
            P("fft", None),
            P("fft", None, None),
            P("fft"),
            P("fft"),
            P(),
            P(),
            P(),
        ),
        out_specs=(P("band", "fft", None), P("band", None, None)),
        check_vma=False,
    )
```

time: 514 us -> 161 us (0.31); the launches traced: 506 us -> 160 us
  local copies, waits for them, and re-layouts: 158 us -> 27.3 us
  blocking collectives: 100 us -> 0 us
  waiting for transfers between devices: 148 us -> 49.1 us
  matrix products: 76.1 us -> 0 us
  Pallas kernels: 0 us -> 49.8 us
  starting transfers between devices: 5.38 us -> 18.1 us
    psum x1 -> x0, waiting for transfers between devices: 82.3 us -> none  [on_device(): coefficients = lax.psum(partial_value, 'fft')]
    dot_general x13 -> x0, matrix products: 76.1 us -> none  [the longest x4 25.2 us: transform(): jnp.einsum(formula, values, weights_table, preferred_element_type=jnp.flo...]
    all_to_all x1 -> x0, blocking collectives: 63.8 us -> none  [on_device(): lax.all_to_all(section_y, 'fft', split_axis=3, concat_axis=1, tiled=True)]
    reshape x5 -> x4, local copies, waits for them, and re-layouts: 66.5 us -> 11 us  [the longest x1 3.53 us: on_device(): potential = local_potential.reshape(NBLK, 8, NG)]
    pallas_call x0 -> x5, Pallas kernels: none -> 49.8 us  [the longest x1 19.7 us: apply_part(): pl.pallas_call(apply_kernel, in_specs=[pl.BlockSpec(memory_space=pltpu.SM...]
    psum x1 -> x0, blocking collectives: 36.5 us -> none  [on_device(): subspace = lax.psum(partial_matrix, 'fft') * (1.0 / (KB * KB * KB))]
    all_to_all x4 -> x0, local copies, waits for them, and re-layouts: 35.5 us -> none  [the longest x2 17.9 us: on_device(): lax.all_to_all(back_z, 'fft', split_axis=4, concat_axis=2, tiled=True)]
    convert_element_type x6 -> x0, local copies, waits for them, and re-layouts: 35.2 us -> none  [the longest x1 13 us: on_device(): real_space = transform('bhcxy,cdhz->bdxyz', lax.all_to_all(section_y, 'ff...]
  transfers between devices with their start and end apart: 3 -> 5, of which waited for: 2 -> 4; matrix products, arithmetic and copies ran while one was open for 20% -> 14% of each run, Pallas kernels for 0% -> 23%
where the time goes in v1:
time: 161 us; the launch traced here: 160 us
  Pallas kernels  49.8 us (31%)
  waiting for transfers between devices  49.1 us (30%)
  local copies, waits for them, and re-layouts  27.3 us (17%)
  starting transfers between devices  18.1 us (11%)
  between operations  14.2 us (9%)
  other arithmetic  1.86 us (1%)
    all_to_all x4, waiting for transfers between devices, exchange(): return lax.all_to_all(array, 'fft', split_axis=0, concat_axis=0, tiled=True)  49.1 us
    pallas_call x1, Pallas kernels, apply_part(): pl.pallas_call(apply_kernel, in_specs=[pl.BlockSpec(memory_space=pltpu.SM...  19.7 us
    all_to_all x4, starting transfers between devices, exchange(): return lax.all_to_all(array, 'fft', split_axis=0, concat_axis=0, tiled=True)  18 us
    pallas_call x1, Pallas kernels, grid_part(): pl.pallas_call(grid_kernel, in_specs=[pl.BlockSpec(memory_space=pltpu.SME...  12.7 us
    pallas_call x1, Pallas kernels, subspace_part(): pl.pallas_call(subspace_kernel, grid=(CHUNKS,), in_specs=[pl.BlockSpec((t...  10.2 us
    unnamed x18, local copies, waits for them, and re-layouts  5.13 us
    transpose x1, local copies, waits for them, and re-layouts, on_device(): projector.reshape(SD, NPROJ, 8, NG).transpose(0, 2, 1, 3)  4.84 us
    pallas_call x1, Pallas kernels, back_transform(): pl.pallas_call(back_kernel, in_specs=[pl.BlockSpec(memory_space=pltpu.SME...  3.71 us
  transfers between devices with their start and end apart: 5, of which 4 were waited for; matrix products, arithmetic and copies ran while one was open for 14% of the time, Pallas kernels for 23%

profile of v1, /device:TPU:160, one launch (start us, length us, event | category | flops | bytes accessed | tf_op | source)
XLA Modules:
  0.0 160.4 jit_solution(6331898276034727632)
XLA Ops:
  7.2 2.9 %reshape.141.wave_ref = bf16[6,4,192,96]{3,2,1,0:T(8,128)(2,1)} reshape(bf16[6,4,18432]{2,1,0:T(4,128)(2,1)} %bitcast.38) | data formatting | bytes 1769472 | tf_op jit(solution)/shard_map/reshape | solution.py:465
  10.2 3.5 %x_transform.1 = bf16[384,2304]{1,0:T(8,128)(2,1)} custom-call(bf16[384,192]{1,0:T(8,128)(2,1)} %constant.103.clone.table_ref, bf16[6,4,192,96]{3,2,1,0:T(8,128)(2,1)} %reshape.141.wave_ref), custom_call_target="tpu_custom_call" | custom-call | tf_op jit(solution)/shard_map/x_transform/pallas_call | solution.py:89
  13.7 1.1 reshape.149.wave0_ref.wave1_ref
  14.8 7.1 %all-to-all-start = ((bf16[16,24,2304]{2,1,0:T(8,128)(2,1)}), bf16[16,24,2304]{2,1,0:T(8,128)(2,1)}, u32[]{:S(2)}, u32[]{:S(2)}) async-start(bf16[16,24,2304]{2,1,0:T(8,128)(2,1)} %bitcast.4), calls=%async_computation | async-start | bytes 3538944 | tf_op jit(solution)/shard_map/all_to_all | solution.py:450
  22.0 3.8 %copy.31 = bf16[128,8,1536]{0,2,1:T(8,128)(2,1)S(1)} copy(bf16[128,8,1536]{2,1,0:T(8,128)(2,1)} %param.24) | data formatting | bytes 6291456 | tf_op args[2]
  25.8 4.8 %copy.32 = bf16[128,8,8,192]{3,2,1,0:T(8,128)(2,1)} copy(bf16[128,8,8,192]{0,3,1,2:T(8,128)(2,1)S(1)} %bitcast.35) | data formatting | bytes 6291456 | tf_op jit(solution)/shard_map/transpose | solution.py:466
  30.6 3.5 %reshape.146.pot_in_ref = f32[288,8,192]{2,1,0:T(8,128)} reshape(f32[12,36864]{1,0:T(8,128)} %param.23) | data formatting | bytes 3538944 | tf_op jit(solution)/shard_map/reshape | solution.py:467
  35.2 1.0 gather_fusion
  37.6 11.3 %all-to-all-done = bf16[16,24,2304]{2,1,0:T(8,128)(2,1)} async-done(((bf16[16,24,2304]{2,1,0:T(8,128)(2,1)}), bf16[16,24,2304]{2,1,0:T(8,128)(2,1)}, u32[]{:S(2)}, u32[]{:S(2)}) %all-to-all-start) | async-done | bytes 1769504 | tf_op jit(solution)/shard_map/all_to_all | solution.py:450
  48.9 12.7 %grid_part.1 = (bf16[16,80,128]{2,1,0:T(8,128)(2,1)}, bf16[288,64,256]{2,1,0:T(8,128)(2,1)}) custom-call(s32[128]{0:T(128)} %slot_ref.3, bf16[192,256]{1,0:T(8,128)(2,1)} %constant.104.clone.ty_ref, bf16[192,512]{1,0:T(8,128)(2,1)} %constant.105.clone.tz_ref, bf16[64,128]{1,0:T(8,128)(2,1)} %constant.109.clone.fold_ref, ...), custom_call_target="tpu_custom_call" | custom-call | tf_op jit(solution)/shard_map/grid_part/pallas_call | solution.py:205
  61.7 3.6 %all-to-all-start.1 = ((bf16[16,80,128]{2,1,0:T(8,128)(2,1)}), bf16[16,80,128]{2,1,0:T(8,128)(2,1)S(1)}, u32[]{:S(2)}, u32[]{:S(2)}) async-start(bf16[16,80,128]{2,1,0:T(8,128)(2,1)} %get-tuple-element.7), calls=%async_computation.1 | async-start | bytes 655360 | tf_op jit(solution)/shard_map/all_to_all | solution.py:450
  65.2 0.7 compare_convert_fusion.kinds_ref
  66.0 8.4 %all-to-all-done.1.exch_ref = bf16[16,80,128]{2,1,0:T(8,128)(2,1)S(1)} async-done(((bf16[16,80,128]{2,1,0:T(8,128)(2,1)}), bf16[16,80,128]{2,1,0:T(8,128)(2,1)S(1)}, u32[]{:S(2)}, u32[]{:S(2)}) %all-to-all-start.1) | async-done | bytes 327712 | tf_op jit(solution)/shard_map/all_to_all | solution.py:450
  74.4 0.8 broadcast_in_dim.36.own_ref
  75.1 19.7 %apply_part.1 = bf16[384,2304]{1,0:T(8,128)(2,1)} custom-call(s32[128]{0:T(128)} %slot_ref.3, bf16[16,80,128]{2,1,0:T(8,128)(2,1)} %copy-done.4, f32[128,128]{1,0:T(8,128)} %broadcast_in_dim.36.own_ref, f32[128,256]{1,0:T(8,128)} %compare_convert_fusion.kinds_ref, f32[128,256]{1,0:T(8,128)} %pad.4.mix_ref, bf16[1024,128]{1,0:T(8,128)(2,1)} %constant.111.clone.rep_ref, ...), custom_call_target="tpu_custom_call" | custom-call | tf_op jit(solution)/shard_map/apply_part/pallas_call | solution.py:325
  94.8 3.9 %all-to-all-start.2 = ((bf16[16,24,2304]{2,1,0:T(8,128)(2,1)}), bf16[16,24,2304]{2,1,0:T(8,128)(2,1)S(1)}, u32[]{:S(2)}, u32[]{:S(2)}) async-start(bf16[16,24,2304]{2,1,0:T(8,128)(2,1)} %bitcast.37), calls=%async_computation.2 | async-start | bytes 3538944 | tf_op jit(solution)/shard_map/all_to_all | solution.py:450
  98.7 24.4 %all-to-all-done.2 = bf16[16,24,2304]{2,1,0:T(8,128)(2,1)S(1)} async-done(((bf16[16,24,2304]{2,1,0:T(8,128)(2,1)}), bf16[16,24,2304]{2,1,0:T(8,128)(2,1)S(1)}, u32[]{:S(2)}, u32[]{:S(2)}) %all-to-all-start.2) | async-done | bytes 1769504 | tf_op jit(solution)/shard_map/all_to_all | solution.py:450
  123.1 1.2 copy-done.2
  124.4 3.7 %back_transform.1 = bf16[6,4,192,96]{3,2,1,0:T(8,128)(2,1)} custom-call(s32[1]{0:T(128)} %bitcast.kz_ref, bf16[192,384]{1,0:T(8,128)(2,1)} %constant.108.clone.table_ref, bf16[384,2304]{1,0:T(8,128)(2,1)} %bitcast.36, bf16[6,4,192,96]{3,2,1,0:T(8,128)(2,1)} %reshape.141.wave_ref, f32[192,96]{1,0:T(8,128)} %constant.113.clone.squares_ref), custom_call_target="tpu_custom_call" | custom-call | tf_op jit(solution)/shard_map/back_transform/pallas_call | solution.py:364
  128.1 3.4 %reshape.150.result0_ref.result1_ref = bf16[24,18432]{1,0:T(8,128)(2,1)} reshape(bf16[6,4,192,96]{3,2,1,0:T(8,128)(2,1)} %back_transform.1) | data formatting | bytes 1769472 | tf_op jit(solution)/shard_map/reshape | solution.py:493
  131.5 10.2 %subspace_part.1 = f32[16,8,128]{2,1,0:T(8,128)} custom-call(bf16[384,18432]{1,0:T(8,128)(2,1)} %all-gather.2.cloned.1.call-done.all0_ref.all1_ref, bf16[384,18432]{1,0:T(8,128)(2,1)} %all-gather.2.cloned.1.call-done.all0_ref.all1_ref, bf16[24,18432]{1,0:T(8,128)(2,1)} %reshape.149.wave0_ref.wave1_ref, bf16[24,18432]{1,0:T(8,128)(2,1)} %reshape.149.wave0_ref.wave1_ref, ...), custom_call_target="tpu_custom_call" | custom-call | tf_op jit(solution)/shard_map/subspace_part/pallas_call | solution.py:424
  141.7 3.5 %all-to-all-start.3 = ((f32[16,8,128]{2,1,0:T(8,128)}), f32[16,8,128]{2,1,0:T(8,128)S(1)}, u32[]{:S(2)}, u32[]{:S(2)}) async-start(f32[16,8,128]{2,1,0:T(8,128)} %subspace_part.1), calls=%async_computation.3 | async-start | bytes 131072 | tf_op jit(solution)/shard_map/all_to_all | solution.py:450
  145.2 2.5 %reshape_reshape.3 = bf16[6,4,18432]{2,1,0:T(4,128)(2,1)} reshape(bf16[6,4,192,96]{3,2,1,0:T(8,128)(2,1)S(1)} %copy-done.1) | data formatting | bytes 1769472 | tf_op jit(solution)/shard_map/reshape;reshape | solution.py:497
  147.7 5.1 %all-to-all-done.3 = f32[16,8,128]{2,1,0:T(8,128)S(1)} async-done(((f32[16,8,128]{2,1,0:T(8,128)}), f32[16,8,128]{2,1,0:T(8,128)S(1)}, u32[]{:S(2)}, u32[]{:S(2)}) %all-to-all-start.3) | async-done | bytes 65568 | tf_op jit(solution)/shard_map/all_to_all | solution.py:450
  (38 shorter events, 3.3 us)
Async XLA Ops:
  7.2 28.1 %copy-start = (s32[1000]{0:T(1024)S(1)}, s32[1000]{0:T(1024)}, u32[]{:S(2)}) copy-start(s32[1000]{0:T(1024)} %param.27) | copy-start | bytes 12004
  7.2 124.3 %all-gather.2.cloned.1.call-start = ((), (), s32[]{:S(2)}) async-start(), calls=%async_computation.4 | async-start | bytes 15040512 | tf_op jit(solution)/shard_map/all_gather | solution.py:483
  7.2 6.4 %copy-start.3 = (bf16[4,6,18432]{2,0,1:T(4,128)(2,1)S(1)}, bf16[4,6,18432]{2,0,1:T(4,128)(2,1)}, u32[]{:S(2)}) copy-start(bf16[4,6,18432]{2,0,1:T(4,128)(2,1)} %param.22) | copy-start | bytes 2654212
  14.8 7.1 %copy-start.6 = (s32[4]{0:T(128)S(1)}, s32[4]{0:T(128)}, u32[]{:S(2)}) copy-start(s32[4]{0:T(128)} %param.28) | copy-start | bytes 52
  14.8 34.1 %all-to-all-start = ((bf16[16,24,2304]{2,1,0:T(8,128)(2,1)}), bf16[16,24,2304]{2,1,0:T(8,128)(2,1)}, u32[]{:S(2)}, u32[]{:S(2)}) async-start(bf16[16,24,2304]{2,1,0:T(8,128)(2,1)} %bitcast.4), calls=%async_computation | async-start | bytes 3538944 | tf_op jit(solution)/shard_map/all_to_all | solution.py:450
  30.6 3.5 %copy-start.5 = (f32[4,8,8]{2,1,0:T(8,128)S(1)}, f32[4,8,8]{2,1,0:T(8,128)}, u32[]{:S(2)}) copy-start(f32[4,8,8]{2,1,0:T(8,128)} %param.29) | copy-start | bytes 3076
  30.6 4.6 %copy-start.7 = (s32[128]{0:T(128)S(1)}, s32[128]{0:T(128)}, u32[]{:S(2)}) copy-start(s32[128]{0:T(128)} %param.26) | copy-start | bytes 1540
  61.7 12.7 %all-to-all-start.1 = ((bf16[16,80,128]{2,1,0:T(8,128)(2,1)}), bf16[16,80,128]{2,1,0:T(8,128)(2,1)S(1)}, u32[]{:S(2)}, u32[]{:S(2)}) async-start(bf16[16,80,128]{2,1,0:T(8,128)(2,1)} %get-tuple-element.7), calls=%async_computation.1 | async-start | bytes 655360 | tf_op jit(solution)/shard_map/all_to_all | solution.py:450
  74.4 0.8 copy-start.4
  94.8 28.3 %all-to-all-start.2 = ((bf16[16,24,2304]{2,1,0:T(8,128)(2,1)}), bf16[16,24,2304]{2,1,0:T(8,128)(2,1)S(1)}, u32[]{:S(2)}, u32[]{:S(2)}) async-start(bf16[16,24,2304]{2,1,0:T(8,128)(2,1)} %bitcast.37), calls=%async_computation.2 | async-start | bytes 3538944 | tf_op jit(solution)/shard_map/all_to_all | solution.py:450
  123.1 1.2 copy-start.2
  131.5 13.7 %copy-start.1 = (bf16[6,4,192,96]{3,2,1,0:T(8,128)(2,1)S(1)}, bf16[6,4,192,96]{3,2,1,0:T(8,128)(2,1)}, u32[]{:S(2)}) copy-start(bf16[6,4,192,96]{3,2,1,0:T(8,128)(2,1)} %back_transform.1) | copy-start | bytes 2654212
  141.7 11.1 %all-to-all-start.3 = ((f32[16,8,128]{2,1,0:T(8,128)}), f32[16,8,128]{2,1,0:T(8,128)S(1)}, u32[]{:S(2)}, u32[]{:S(2)}) async-start(f32[16,8,128]{2,1,0:T(8,128)} %subspace_part.1), calls=%async_computation.3 | async-start | bytes 131072 | tf_op jit(solution)/shard_map/all_to_all | solution.py:450
Sparse Core Ops, SparseCore 0:
  14.9 82.2 all-gather.1

commit v2 on v1

--- a/solution.py
+++ b/solution.py
@@ -28,7 +28,7 @@
 F32 = jnp.float32
 HIGH = lax.Precision.HIGHEST
 MIB = 1024 * 1024
-PLANE_UNROLL = 2
+PLANE_UNROLL = 3
 
 
 def table(scaling, direction):
@@ -89,7 +89,7 @@
     return pl.pallas_call(
         x_kernel,
         out_shape=jax.ShapeDtypeStruct((ND * DX, LANES), BF),
-        compiler_params=pltpu.CompilerParams(vmem_limit_bytes=60 * MIB),
+        compiler_params=pltpu.CompilerParams(vmem_limit_bytes=24 * MIB),
         name="x_transform",
     )(table_x, wave)
 
@@ -114,26 +114,18 @@
 
 
 def grid_kernel(
-    slot_ref, ty_ref, tz_ref, fold_ref, sums_ref, ids_ref, in_ref, proj_in_ref,
+    slot_ref, ty_ref, tz_ref, fold_ref, ids_ref, in_ref, proj_in_ref,
     exch_ref, real_ref,
-    held_ref, proj_ref, wide_ref, space_ref, terms_ref, in_sems, proj_sem, out_sems,
+    proj_ref, wide_ref, space_ref, terms_ref, proj_sem, out_sems,
 ):
-    def columns_in(h):
-        columns = pl.ds(h * GROUP, GROUP)
-        return pltpu.make_async_copy(in_ref.at[:, columns], held_ref.at[h], in_sems.at[h])
-
     def plane_out(plane):
         blocks = pl.ds(plane * (NG // 8), NG // 8)
         return pltpu.make_async_copy(space_ref.at[blocks], real_ref.at[blocks], out_sems.at[plane])
 
-    for h in range(HD):
-        columns_in(h).start()
     projector_in = pltpu.make_async_copy(proj_in_ref, proj_ref, proj_sem)
     projector_in.start()
-    for h in range(HD):
-        columns_in(h).wait()
-        for v in range(3):
-            wide_ref[3 * h + v] = held_ref[h, :, v * 128 : v * 128 + 128].astype(F32)
+    for t in range(TILES):
+        wide_ref[t] = in_ref[:, t * 128 : t * 128 + 128].astype(F32)
 
     def plane_step(plane, carry):
         pieces = []
@@ -186,7 +178,8 @@
     folded = dot(high, fold_ref[...]) + dot(low, fold_ref[...])
     keep = iota(folded.shape, 0) % 8 == iota(folded.shape, 1) % 64 // 8
     folded = jnp.where(keep, folded, 0.0).astype(BF)
-    ordered = dot(sums_ref[...], folded)
+    sums = jnp.where(iota((SD, 1024), 1) // 8 == iota((SD, 1024), 0), 1.0, 0.0).astype(BF)
+    ordered = dot(sums, folded)
     packed = jnp.where(iota((64, 128), 1) < 64, ordered[:64], ordered[64:]).astype(BF)
     for k in range(ND):
         exch_ref[k, 0:64, :] = packed
@@ -200,36 +193,33 @@
     for bc in range(8):
         for y in range(8):
             fold[bc * 8 + y, bc::8] = 1.0
-    sums = (np.arange(1024)[None, :] // 8 == np.arange(128)[:, None]).astype(np.float32)
     vmem, anywhere = pl.BlockSpec(memory_space=pltpu.VMEM), pl.BlockSpec(memory_space=pl.ANY)
     return pl.pallas_call(
         grid_kernel,
-        in_specs=[pl.BlockSpec(memory_space=pltpu.SMEM)] + [vmem] * 5 + [anywhere] * 2,
+        in_specs=[pl.BlockSpec(memory_space=pltpu.SMEM)] + [vmem] * 5 + [anywhere],
         out_specs=[vmem, anywhere],
         out_shape=[
             jax.ShapeDtypeStruct((ND, 80, 128), BF),
             jax.ShapeDtypeStruct((NBLK, 64, 256), BF),
         ],
         scratch_shapes=[
-            pltpu.VMEM((HD, ND * DX, GROUP), BF),
             pltpu.VMEM((SD, 64, NG), BF),
             pltpu.VMEM((TILES, ND * DX, 128), F32),
             pltpu.VMEM((NBLK, 64, 256), BF),
             pltpu.VMEM((SD * 8, 64), F32),
-            pltpu.SemaphoreType.DMA((HD,)),
             pltpu.SemaphoreType.DMA,
             pltpu.SemaphoreType.DMA((XD,)),
         ],
-        compiler_params=pltpu.CompilerParams(vmem_limit_bytes=60 * MIB),
+        compiler_params=pltpu.CompilerParams(vmem_limit_bytes=58 * MIB),
         name="grid_part",
     )(
-        slot_block, tables["by"], tables["bz"], jnp.asarray(fold, BF), jnp.asarray(sums, BF), ids,
+        slot_block, tables["by"], tables["bz"], jnp.asarray(fold, BF), ids,
         received, projector,
     )
 
 
 def apply_kernel(
-    slot_ref, exch_ref, own_ref, kinds_ref, mix_ref, rep_ref, spread_ref, tz_ref, ty_ref,
+    slot_ref, exch_ref, own_ref, kinds_ref, mix_ref, spread_ref, tz_ref, ty_ref,
     real_in_ref, pot_in_ref, proj_in_ref,
     out_ref,
     real_ref, pot_ref, proj_ref, field_ref, wide_ref, weight_ref, real_sems, pot_sems, proj_sem,
@@ -262,7 +252,8 @@
     mixed = mixed * kinds_ref[...]
     mixed = mixed[:, :128] + mixed[:, 128:]
     weighted = (mixed + pltpu.roll(mixed, 64, 1)).astype(BF)
-    spread = dot(rep_ref[...], weighted)
+    repeat = jnp.where(iota((1024, SD), 0) // 8 == iota((1024, SD), 1), 1.0, 0.0).astype(BF)
+    spread = dot(repeat, weighted)
     keep = iota(spread.shape, 0) % 8 == iota(spread.shape, 1) % 8
     spread = jnp.where(keep, spread, 0.0).astype(BF)
     weight_ref[...] = dot(spread, spread_ref[...])
@@ -317,14 +308,13 @@
 
 
 def apply_part(tables, exchanged, own, kinds, mix, real_space, potential, projector, slot_block):
-    rep = (np.arange(1024)[:, None] // 8 == np.arange(128)[None, :]).astype(np.float32)
     spread = np.zeros((128, 64), np.float32)
     for p in range(8):
         spread[p * 8 : p * 8 + 8, p::8] = 1.0
     vmem, anywhere = pl.BlockSpec(memory_space=pltpu.VMEM), pl.BlockSpec(memory_space=pl.ANY)
     return pl.pallas_call(
         apply_kernel,
-        in_specs=[pl.BlockSpec(memory_space=pltpu.SMEM)] + [vmem] * 8 + [anywhere] * 3,
+        in_specs=[pl.BlockSpec(memory_space=pltpu.SMEM)] + [vmem] * 7 + [anywhere] * 3,
         out_specs=vmem,
         out_shape=jax.ShapeDtypeStruct((ND * DX, LANES), BF),
         scratch_shapes=[
@@ -338,76 +328,93 @@
             pltpu.SemaphoreType.DMA((XD,)),
             pltpu.SemaphoreType.DMA,
         ],
-        compiler_params=pltpu.CompilerParams(vmem_limit_bytes=60 * MIB),
+        compiler_params=pltpu.CompilerParams(vmem_limit_bytes=59 * MIB),
         name="apply_part",
     )(
-        slot_block, exchanged, own, kinds, mix, jnp.asarray(rep, BF), jnp.asarray(spread, BF),
+        slot_block, exchanged, own, kinds, mix, jnp.asarray(spread, BF),
         tables["cz"], tables["cy"], real_space, potential, projector,
     )
 
 
-def back_kernel(kz_ref, table_ref, in_ref, wave_ref, squares_ref, out_ref):
+ROWS = HD * NBD
+CHUNK = 2304
+CHUNKS = KB * KB // CHUNK
+HALF = KB * KB
+
+
+def tail_kernel(
+    kz_ref, table_ref, fold0_ref, fold1_ref, rows_ref, in_ref, wave_in_ref, all_in_ref,
+    result_ref, out_ref,
+    wave_ref, all_ref, spectrum_ref, wave_sem, all_sems,
+):
+    def chunk_in(c, i):
+        columns = pl.ds(c * HALF + i * CHUNK, CHUNK)
+        return pltpu.make_async_copy(
+            all_in_ref.at[:, columns], all_ref.at[c, i], all_sems.at[c, i]
+        )
+
+    wave_in = pltpu.make_async_copy(wave_in_ref, wave_ref, wave_sem)
+    wave_in.start()
+    for i in range(CHUNKS):
+        for c in range(2):
+            chunk_in(c, i).start()
     for h in range(HD):
-        kz = (kz_ref[0] + (h - KB // 2)).astype(F32)
-        energy = (squares_ref[...] + kz * kz) * (2.0 / (KB * KB))
         spectrum = dot(table_ref[...], in_ref[:, h * GROUP : (h + 1) * GROUP])
         parts = split_bands(spectrum[:, :128], spectrum[:, 128:256], spectrum[:, 256:])
         for b in range(NBD):
-            own = wave_ref[h, b].astype(F32)
-            out_ref[h, b] = (parts[b][:, :KB] + energy * own).astype(BF)
-
-
-def back_transform(table_x, first_kz, received, wave):
-    signed = np.arange(KB) - KB // 2
-    squares = (signed * signed)[:, None] + (signed * signed)[None, :]
-    squares = np.tile(squares, (2, 1)).astype(np.float32)
-    return pl.pallas_call(
-        back_kernel,
-        in_specs=[pl.BlockSpec(memory_space=pltpu.SMEM)]
-        + [pl.BlockSpec(memory_space=pltpu.VMEM)] * 4,
-        out_shape=jax.ShapeDtypeStruct((HD, NBD, 2 * KB, KB), BF),
-        compiler_params=pltpu.CompilerParams(vmem_limit_bytes=60 * MIB),
-        name="back_transform",
-    )(first_kz, table_x, received, wave, jnp.asarray(squares))
-
-
-ROWS = HD * NBD
-CHUNK = 2304
-CHUNKS = KB * KB // CHUNK
-
-
-def subspace_kernel(
-    all0_ref, all1_ref, wave0_ref, wave1_ref, result0_ref, result1_ref,
-    fold0_ref, fold1_ref, rows_ref,
-    out_ref,
-    acc0, acc1,
-):
-    step = pl.program_id(0)
-
-    @pl.when(step == 0)
-    def _():
-        acc0[...] = jnp.zeros_like(acc0)
-        acc1[...] = jnp.zeros_like(acc1)
-
-    own = [wave0_ref, result0_ref, wave1_ref, result1_ref]
-    right = jnp.concatenate([ref[...].astype(F32) for ref in own], axis=0).astype(BF)
-    acc0[...] += dot_nt(all0_ref[...], right)
-    acc1[...] += dot_nt(all1_ref[...], right)
-
-    @pl.when(step == CHUNKS - 1)
-    def _():
-        shape = acc0.shape
-        keep = iota(shape, 0) % ROWS // NBD == iota(shape, 1) % ROWS // NBD
-        folded = jnp.dot(
-            jnp.where(keep, acc0[...], 0.0), fold0_ref[...], precision=HIGH
-        ) + jnp.dot(jnp.where(keep, acc1[...], 0.0), fold1_ref[...], precision=HIGH)
-        turned = jnp.dot(folded.T[:16], rows_ref[...], precision=HIGH)
-        packed = jnp.where(iota((8, 128), 1) < 64, turned[:8], turned[8:])
-        for k in range(ND):
-            out_ref[k] = packed
-
-
-def subspace_part(everything, wave, result):
+            first = (h * NBD + b) * 2 * KB
+            spectrum_ref[first : first + 2 * KB, :] = parts[b]
+    wave_in.wait()
+
+    kz = kz_ref[0] + iota((ROWS, 128), 0) // NBD - KB // 2
+    kz = (kz * kz).astype(F32)
+    entry = [iota((ROWS, 128), 1) + v * 128 for v in range(3)]
+    row = [(e >= KB).astype(F32) + (e >= 2 * KB).astype(F32) + (e >= 3 * KB).astype(F32) for e in entry]
+    ky = [entry[v].astype(F32) - KB * row[v] - KB // 2 for v in range(3)]
+    fixed = [ky[v] * ky[v] + kz for v in range(3)]
+
+    def flatten(group, carry):
+        pieces = [
+            spectrum_ref[pl.ds(group * 4 + v, ROWS, stride=2 * KB), :] for v in range(4)
+        ]
+        joined = join_bands(pieces)
+        start = pl.multiple_of(group * GROUP, GROUP)
+        first_kx = (lax.rem(group, KB // 4) * 4 - KB // 2).astype(F32)
+        for v in range(3):
+            columns = pl.ds(start + v * 128, 128)
+            kx = row[v] + first_kx
+            energy = (kx * kx + fixed[v]) * (2.0 / (KB * KB))
+            value = joined[v] + energy * wave_ref[:, columns].astype(F32)
+            result_ref[:, columns] = value.astype(BF)
+        return carry
+
+    lax.fori_loop(0, 2 * KB // 4, flatten, 0, unroll=4)
+
+    total0, total1 = None, None
+    for i in range(CHUNKS):
+        low, high = slice(i * CHUNK, (i + 1) * CHUNK), slice(HALF + i * CHUNK, HALF + (i + 1) * CHUNK)
+        right = [wave_ref[:, low], result_ref[:, low], wave_ref[:, high], result_ref[:, high]]
+        right = jnp.concatenate([part.astype(F32) for part in right], axis=0).astype(BF)
+        chunk_in(0, i).wait()
+        term0 = dot_nt(right, all_ref[0, i])
+        chunk_in(1, i).wait()
+        term1 = dot_nt(right, all_ref[1, i])
+        total0 = term0 if total0 is None else total0 + term0
+        total1 = term1 if total1 is None else total1 + term1
+
+    total0, total1 = total0.T, total1.T
+    shape = total0.shape
+    keep = iota(shape, 0) % ROWS // NBD == iota(shape, 1) % ROWS // NBD
+    folded = jnp.dot(jnp.where(keep, total0, 0.0), fold0_ref[...], precision=HIGH) + jnp.dot(
+        jnp.where(keep, total1, 0.0), fold1_ref[...], precision=HIGH
+    )
+    turned = jnp.dot(folded.T[:16], rows_ref[...], precision=HIGH)
+    packed = jnp.where(iota((8, 128), 1) < 64, turned[:8], turned[8:])
+    for k in range(ND):
+        out_ref[k] = packed
+
+
+def tail_part(table_x, first_kz, received, everything, wave):
     fold0 = np.zeros((2, 2, HD, NBD, 128), np.float32)
     fold1 = np.zeros((2, 2, HD, NBD, 128), np.float32)
     for k in range(2):
@@ -420,29 +427,27 @@
     row = np.arange(total)
     band = row // ROWS * NBD + row % NBD
     rows = (band[:, None] == np.arange(128)[None, :] % 64).astype(np.float32)
-    whole = lambda *shape: pl.BlockSpec(shape, lambda i: (0,) * len(shape))
+    vmem, anywhere = pl.BlockSpec(memory_space=pltpu.VMEM), pl.BlockSpec(memory_space=pl.ANY)
     return pl.pallas_call(
-        subspace_kernel,
-        grid=(CHUNKS,),
-        in_specs=[
-            pl.BlockSpec((total, CHUNK), lambda i: (0, i)),
-            pl.BlockSpec((total, CHUNK), lambda i: (0, CHUNKS + i)),
-            pl.BlockSpec((ROWS, CHUNK), lambda i: (0, i)),
-            pl.BlockSpec((ROWS, CHUNK), lambda i: (0, CHUNKS + i)),
-            pl.BlockSpec((ROWS, CHUNK), lambda i: (0, i)),
-            pl.BlockSpec((ROWS, CHUNK), lambda i: (0, CHUNKS + i)),
-            whole(4 * ROWS, 128),
-            whole(4 * ROWS, 128),
-            whole(total, 128),
+        tail_kernel,
+        in_specs=[pl.BlockSpec(memory_space=pltpu.SMEM)] + [vmem] * 5 + [anywhere] * 2,
+        out_specs=[vmem, vmem],
+        out_shape=[
+            jax.ShapeDtypeStruct((ROWS, PLANE), BF),
+            jax.ShapeDtypeStruct((ND, 8, 128), F32),
         ],
-        out_specs=whole(ND, 8, 128),
-        out_shape=jax.ShapeDtypeStruct((ND, 8, 128), F32),
-        scratch_shapes=[pltpu.VMEM((total, 4 * ROWS), F32), pltpu.VMEM((total, 4 * ROWS), F32)],
-        compiler_params=pltpu.CompilerParams(vmem_limit_bytes=60 * MIB),
-        name="subspace_part",
+        scratch_shapes=[
+            pltpu.VMEM((ROWS, PLANE), BF),
+            pltpu.VMEM((2, CHUNKS, total, CHUNK), BF),
+            pltpu.VMEM((ROWS * 2 * KB, 128), F32),
+            pltpu.SemaphoreType.DMA,
+            pltpu.SemaphoreType.DMA((2, CHUNKS)),
+        ],
+        compiler_params=pltpu.CompilerParams(vmem_limit_bytes=50 * MIB),
+        name="tail_part",
     )(
-        everything, everything, wave, wave, result, result,
-        jnp.asarray(fold0.reshape(-1, 128)), jnp.asarray(fold1.reshape(-1, 128)), jnp.asarray(rows),
+        first_kz, table_x, jnp.asarray(fold0.reshape(-1, 128)), jnp.asarray(fold1.reshape(-1, 128)),
+        jnp.asarray(rows), received, wave, everything,
     )
 
 
@@ -481,7 +486,10 @@
     sent, rows = lax.optimization_barrier((sent, rows))
     flat = rows.reshape(ROWS, PLANE)
     everything = lax.all_gather(flat, "band", axis=0, tiled=True)
+    prepared = (ids, own_ids, kinds, mix, projector, potential)
     received = exchange(sent.reshape(ND, DX, LANES)).reshape(ND * DX, LANES)
+    received, prepared = lax.optimization_barrier((received, prepared))
+    ids, own_ids, kinds, mix, projector, potential = prepared
     terms, real_space = grid_part(tables, received, projector, slot_block, ids)
     exchanged = exchange(terms)
     sent = apply_part(
@@ -489,9 +497,7 @@
     )
     received = exchange(sent.reshape(ND, DX, LANES)).reshape(ND * DX, LANES)
     first_kz = (lax.axis_index("fft") * HD).astype(jnp.int32).reshape(1)
-    result = back_transform(tables["d"], first_kz, received, wave)
-    result = result.reshape(ROWS, PLANE)
-    partial = subspace_part(everything, flat, result)
+    result, partial = tail_part(tables["d"], first_kz, received, everything, flat)
     summed = exchange(partial).sum(axis=0) * (1.0 / (KB * KB * KB))
     subspace = summed.reshape(8, 2, 64).transpose(1, 0, 2).reshape(NBD, 4, 64)
     result_coeffs = result.reshape(HD, NBD, PLANE).transpose(1, 0, 2)

time: 161 us -> 153 us (0.950)
  blocking collectives: 0 us -> 13.3 us
  waiting for transfers between devices: 49.1 us -> 40.8 us
  Pallas kernels: 49.8 us -> 42.7 us
  starting transfers between devices: 18.1 us -> 14.7 us
  local copies, waits for them, and re-layouts: 27.3 us -> 25.3 us
    all_to_all x0 -> x1, blocking collectives: none -> 13.3 us  [exchange(): return lax.all_to_all(array, 'fft', split_axis=0, concat_axis=0, tiled=True)]
    all_to_all x4 -> x3, waiting for transfers between devices: 49.1 us -> 40.8 us  [exchange(): return lax.all_to_all(array, 'fft', split_axis=0, concat_axis=0, tiled=True)]
    pallas_call x2 -> x1, Pallas kernels: 13.9 us -> 9.97 us  [tail_part(): pl.pallas_call(tail_kernel, in_specs=[pl.BlockSpec(memory_space=pltpu.SME...]
    unnamed x18 -> x26, local copies, waits for them, and re-layouts: 5.13 us -> 8.86 us
    all_to_all x4 -> x3, starting transfers between devices: 18 us -> 14.6 us  [exchange(): return lax.all_to_all(array, 'fft', split_axis=0, concat_axis=0, tiled=True)]
    another operation x1 -> x0, local copies, waits for them, and re-layouts: 2.53 us -> none  [on_device(): result_coeffs = result.reshape(HD, NBD, PLANE).transpose(1, 0, 2)]
    reshape x1, local copies, waits for them, and re-layouts: 3.44 us -> 1.23 us  [on_device(): result_coeffs = result.reshape(HD, NBD, PLANE).transpose(1, 0, 2)]
  transfers between devices with their start and end apart: 5 -> 4, of which waited for: 4 -> 3; matrix products, arithmetic and copies ran while one was open for 14% -> 12% of each run, Pallas kernels for 23% -> 20%
where the time goes in v2:
time: 153 us
  Pallas kernels  42.7 us (28%)
  waiting for transfers between devices  40.8 us (27%)
  local copies, waits for them, and re-layouts  25.3 us (17%)
  starting transfers between devices  14.7 us (10%)
  between operations  14.2 us (9%)
  blocking collectives  13.3 us (9%)
  other arithmetic  1.84 us (1%)
    all_to_all x3, waiting for transfers between devices, exchange(): return lax.all_to_all(array, 'fft', split_axis=0, concat_axis=0, tiled=True)  40.8 us
    pallas_call x1, Pallas kernels, apply_part(): pl.pallas_call(apply_kernel, in_specs=[pl.BlockSpec(memory_space=pltpu.SM...  19.1 us
    all_to_all x3, starting transfers between devices, exchange(): return lax.all_to_all(array, 'fft', split_axis=0, concat_axis=0, tiled=True)  14.6 us
    all_to_all x1, blocking collectives, exchange(): return lax.all_to_all(array, 'fft', split_axis=0, concat_axis=0, tiled=True)  13.3 us
    pallas_call x1, Pallas kernels, grid_part(): pl.pallas_call(grid_kernel, in_specs=[pl.BlockSpec(memory_space=pltpu.SME...  11.5 us
    pallas_call x1, Pallas kernels, tail_part(): pl.pallas_call(tail_kernel, in_specs=[pl.BlockSpec(memory_space=pltpu.SME...  9.97 us
    unnamed x26, local copies, waits for them, and re-layouts  8.86 us
    transpose x1, local copies, waits for them, and re-layouts, on_device(): projector.reshape(SD, NPROJ, 8, NG).transpose(0, 2, 1, 3)  4.85 us
  transfers between devices with their start and end apart: 4, of which 3 were waited for; matrix products, arithmetic and copies ran while one was open for 12% of the time, Pallas kernels for 20%

profile of v2, /device:TPU:160, one launch (start us, length us, event | category | flops | bytes accessed | tf_op | source)
XLA Modules:
  0.0 152.7 jit_solution(17013164364312594870)
XLA Ops:
  7.2 2.1 %reshape.141.wave_ref = bf16[6,4,192,96]{3,2,1,0:T(8,128)(2,1)S(1)} reshape(bf16[6,4,18432]{2,1,0:T(4,128)(2,1)} %bitcast.34) | data formatting | bytes 1769472 | tf_op jit(solution)/shard_map/reshape | solution.py:470
  9.4 0.9 copy-done.3
  10.3 2.1 %x_transform.1 = bf16[384,2304]{1,0:T(8,128)(2,1)} custom-call(bf16[384,192]{1,0:T(8,128)(2,1)S(1)} %copy-done.3, bf16[6,4,192,96]{3,2,1,0:T(8,128)(2,1)S(1)} %reshape.141.wave_ref), custom_call_target="tpu_custom_call" | custom-call | tf_op jit(solution)/shard_map/x_transform/pallas_call | solution.py:89
  12.4 1.1 reshape.149.wave_in_ref
  13.5 7.1 %all-to-all-start = ((bf16[16,24,2304]{2,1,0:T(8,128)(2,1)}), bf16[16,24,2304]{2,1,0:T(8,128)(2,1)}, u32[]{:S(2)}, u32[]{:S(2)}) async-start(bf16[16,24,2304]{2,1,0:T(8,128)(2,1)} %bitcast.2), calls=%async_computation | async-start | bytes 3538944 | tf_op jit(solution)/shard_map/all_to_all | solution.py:455
  20.6 3.8 %copy.30 = bf16[128,8,1536]{0,2,1:T(8,128)(2,1)S(1)} copy(bf16[128,8,1536]{2,1,0:T(8,128)(2,1)} %param.21) | data formatting | bytes 6291456 | tf_op args[2]
  24.4 4.8 %copy.31 = bf16[128,8,8,192]{3,2,1,0:T(8,128)(2,1)} copy(bf16[128,8,8,192]{0,3,1,2:T(8,128)(2,1)S(1)} %bitcast.32) | data formatting | bytes 6291456 | tf_op jit(solution)/shard_map/transpose | solution.py:471
  29.3 3.4 %reshape.146.pot_in_ref = f32[288,8,192]{2,1,0:T(8,128)} reshape(f32[12,36864]{1,0:T(8,128)} %param.20) | data formatting | bytes 3538944 | tf_op jit(solution)/shard_map/reshape | solution.py:472
  33.8 1.0 gather_fusion
  36.2 0.7 compare_convert_fusion.kinds_ref
  36.9 10.7 %all-to-all-done = bf16[16,24,2304]{2,1,0:T(8,128)(2,1)} async-done(((bf16[16,24,2304]{2,1,0:T(8,128)(2,1)}), bf16[16,24,2304]{2,1,0:T(8,128)(2,1)}, u32[]{:S(2)}, u32[]{:S(2)}) %all-to-all-start) | async-done | bytes 1769504 | tf_op jit(solution)/shard_map/all_to_all | solution.py:455
  48.3 11.5 %grid_part.1 = (bf16[16,80,128]{2,1,0:T(8,128)(2,1)}, bf16[288,64,256]{2,1,0:T(8,128)(2,1)}) custom-call(s32[128]{0:T(128)} %slot_ref.3, bf16[192,256]{1,0:T(8,128)(2,1)} %constant.98.clone.ty_ref, bf16[192,512]{1,0:T(8,128)(2,1)} %constant.99.clone.tz_ref, bf16[64,128]{1,0:T(8,128)(2,1)} %constant.103.clone.fold_ref, ...), custom_call_target="tpu_custom_call" | custom-call | tf_op jit(solution)/shard_map/grid_part/pallas_call | solution.py:197
  59.9 13.3 %all_to_all.20.exch_ref = bf16[16,80,128]{2,1,0:T(8,128)(2,1)} all-to-all(bf16[16,80,128]{2,1,0:T(8,128)(2,1)} %get-tuple-element.19), channel_id=1, replica_groups=mesh['band'=16,'fft'=16] {'fft'}, dimensions={0} | all-to-all | bytes 655360 | tf_op jit(solution)/shard_map/all_to_all | solution.py:455
  73.1 19.1 %apply_part.1 = bf16[384,2304]{1,0:T(8,128)(2,1)} custom-call(s32[128]{0:T(128)} %slot_ref.3, bf16[16,80,128]{2,1,0:T(8,128)(2,1)} %all_to_all.20.exch_ref, f32[128,128]{1,0:T(8,128)} %broadcast_in_dim.36.own_ref, f32[128,256]{1,0:T(8,128)} %compare_convert_fusion.kinds_ref, f32[128,256]{1,0:T(8,128)} %pad.4.mix_ref, ...), custom_call_target="tpu_custom_call" | custom-call | tf_op jit(solution)/shard_map/apply_part/pallas_call | solution.py:315
  92.3 4.0 %all-to-all-start.2 = ((bf16[16,24,2304]{2,1,0:T(8,128)(2,1)}), bf16[16,24,2304]{2,1,0:T(8,128)(2,1)S(1)}, u32[]{:S(2)}, u32[]{:S(2)}) async-start(bf16[16,24,2304]{2,1,0:T(8,128)(2,1)} %bitcast.33), calls=%async_computation.2 | async-start | bytes 3538944 | tf_op jit(solution)/shard_map/all_to_all | solution.py:455
  96.3 23.7 %all-to-all-done.2 = bf16[16,24,2304]{2,1,0:T(8,128)(2,1)S(1)} async-done(((bf16[16,24,2304]{2,1,0:T(8,128)(2,1)}), bf16[16,24,2304]{2,1,0:T(8,128)(2,1)S(1)}, u32[]{:S(2)}, u32[]{:S(2)}) %all-to-all-start.2) | async-done | bytes 1769504 | tf_op jit(solution)/shard_map/all_to_all | solution.py:455
  120.0 0.9 copy-done.2
  120.9 0.9 copy-done.4
  121.8 0.8 copy-done.6
  122.6 0.8 copy-done.7
  123.4 10.0 %tail_part.1 = (bf16[24,18432]{1,0:T(8,128)(2,1)S(1)}, f32[16,8,128]{2,1,0:T(8,128)S(1)}) custom-call(s32[1]{0:T(128)} %bitcast.kz_ref, bf16[192,384]{1,0:T(8,128)(2,1)S(1)} %copy-done.4, f32[96,128]{1,0:T(8,128)S(1)} %copy-done.6, f32[96,128]{1,0:T(8,128)S(1)} %copy-done.7, f32[384,128]{1,0:T(8,128)S(1)} %copy-done.2, bf16[384,2304]{1,0:T(8,128)(2,1)S(1)} %bitcast.29, ...), custom_call_target="tpu_custom_call" | custom-call | tf_op jit(solution)/shard_map/tail_part/pallas_call | solution.py:431
  134.0 3.5 %all-to-all-start.3 = ((f32[16,8,128]{2,1,0:T(8,128)}), f32[16,8,128]{2,1,0:T(8,128)S(1)}, u32[]{:S(2)}, u32[]{:S(2)}) async-start(f32[16,8,128]{2,1,0:T(8,128)} %copy-done.5), calls=%async_computation.3 | async-start | bytes 131072 | tf_op jit(solution)/shard_map/all_to_all | solution.py:455
  137.5 1.2 reshape.150
  138.8 6.4 %all-to-all-done.3 = f32[16,8,128]{2,1,0:T(8,128)S(1)} async-done(((f32[16,8,128]{2,1,0:T(8,128)}), f32[16,8,128]{2,1,0:T(8,128)S(1)}, u32[]{:S(2)}, u32[]{:S(2)}) %all-to-all-start.3) | async-done | bytes 65568 | tf_op jit(solution)/shard_map/all_to_all | solution.py:455
  (43 shorter events, 4.6 us)
Async XLA Ops:
  7.2 26.7 %copy-start = (s32[1000]{0:T(1024)S(1)}, s32[1000]{0:T(1024)}, u32[]{:S(2)}) copy-start(s32[1000]{0:T(1024)} %param.24) | copy-start | bytes 12004
  7.2 112.8 %all-gather.2.cloned.1.call-start = ((), (), s32[]{:S(2)}) async-start(), calls=%async_computation.4 | async-start | bytes 15040512 | tf_op jit(solution)/shard_map/all_gather | solution.py:488
  7.2 5.1 %copy-start.8 = (bf16[4,6,18432]{2,0,1:T(4,128)(2,1)S(1)}, bf16[4,6,18432]{2,0,1:T(4,128)(2,1)}, u32[]{:S(2)}) copy-start(bf16[4,6,18432]{2,0,1:T(4,128)(2,1)} %param.19) | copy-start | bytes 2654212
  9.3 0.9 copy-start.3
  13.5 34.1 %all-to-all-start = ((bf16[16,24,2304]{2,1,0:T(8,128)(2,1)}), bf16[16,24,2304]{2,1,0:T(8,128)(2,1)}, u32[]{:S(2)}, u32[]{:S(2)}) async-start(bf16[16,24,2304]{2,1,0:T(8,128)(2,1)} %bitcast.2), calls=%async_computation | async-start | bytes 3538944 | tf_op jit(solution)/shard_map/all_to_all | solution.py:455
  29.3 3.4 %copy-start.9 = (f32[4,8,8]{2,1,0:T(8,128)S(1)}, f32[4,8,8]{2,1,0:T(8,128)}, u32[]{:S(2)}) copy-start(f32[4,8,8]{2,1,0:T(8,128)} %param.26) | copy-start | bytes 3076
  29.3 3.5 %copy-start.10 = (s32[4]{0:T(128)S(1)}, s32[4]{0:T(128)}, u32[]{:S(2)}) copy-start(s32[4]{0:T(128)} %param.25) | copy-start | bytes 52
  29.3 4.5 %copy-start.11 = (s32[128]{0:T(128)S(1)}, s32[128]{0:T(128)}, u32[]{:S(2)}) copy-start(s32[128]{0:T(128)} %param.23) | copy-start | bytes 1540
  92.2 27.8 %copy-start.1 = (bf16[24,18432]{1,0:T(8,128)(2,1)S(1)}, bf16[24,18432]{1,0:T(8,128)(2,1)}, u32[]{:S(2)}) copy-start(bf16[24,18432]{1,0:T(8,128)(2,1)} %reshape.149.wave_in_ref) | copy-start | bytes 2654212
  92.3 27.7 %all-to-all-start.2 = ((bf16[16,24,2304]{2,1,0:T(8,128)(2,1)}), bf16[16,24,2304]{2,1,0:T(8,128)(2,1)S(1)}, u32[]{:S(2)}, u32[]{:S(2)}) async-start(bf16[16,24,2304]{2,1,0:T(8,128)(2,1)} %bitcast.33), calls=%async_computation.2 | async-start | bytes 3538944 | tf_op jit(solution)/shard_map/all_to_all | solution.py:455
  120.0 0.9 copy-start.2
  120.9 0.9 copy-start.4
  121.8 0.8 copy-start.6
  122.6 0.8 copy-start.7
  133.4 0.6 copy-start.5
  134.0 11.1 %all-to-all-start.3 = ((f32[16,8,128]{2,1,0:T(8,128)}), f32[16,8,128]{2,1,0:T(8,128)S(1)}, u32[]{:S(2)}, u32[]{:S(2)}) async-start(f32[16,8,128]{2,1,0:T(8,128)} %copy-done.5), calls=%async_computation.3 | async-start | bytes 131072 | tf_op jit(solution)/shard_map/all_to_all | solution.py:455
Sparse Core Ops, SparseCore 0:
  13.6 82.2 all-gather.1

commit v3 on v2

--- a/solution.py
+++ b/solution.py
@@ -23,12 +23,13 @@
 LANES = HD * NBD * KB
 TILES = LANES // 128
 GROUP = NBD * KB
+ROWS = HD * NBD
 PLANE = 2 * KB * KB
 BF = jnp.bfloat16
 F32 = jnp.float32
 HIGH = lax.Precision.HIGHEST
 MIB = 1024 * 1024
-PLANE_UNROLL = 3
+PLANE_UNROLL = 6
 
 
 def table(scaling, direction):
@@ -171,7 +172,7 @@
         terms_ref[pl.ds(pl.multiple_of(s * 8, 8), 8), :] = total
         return carry
 
-    lax.fori_loop(0, SD, slot, 0, unroll=8)
+    lax.fori_loop(0, SD, slot, 0, unroll=32)
     terms = terms_ref[...]
     high = terms.astype(BF)
     low = (terms - high.astype(F32)).astype(BF)
@@ -219,10 +220,12 @@
 
 
 def apply_kernel(
-    slot_ref, exch_ref, own_ref, kinds_ref, mix_ref, spread_ref, tz_ref, ty_ref,
+    slot_ref, exch_in, ids_in, kinds_in, mix_in, spread_in, tz_in, ty_in,
     real_in_ref, pot_in_ref, proj_in_ref,
     out_ref,
-    real_ref, pot_ref, proj_ref, field_ref, wide_ref, weight_ref, real_sems, pot_sems, proj_sem,
+    exch_ref, ids_ref, kinds_ref, mix_ref, spread_ref, tz_ref, ty_ref,
+    real_ref, pot_ref, proj_ref, field_ref, wide_ref, weight_ref,
+    small_sems, real_sems, pot_sems, proj_sem,
 ):
     def plane_in(plane):
         blocks = pl.ds(plane * (NG // 8), NG // 8)
@@ -231,19 +234,31 @@
             pltpu.make_async_copy(pot_in_ref.at[blocks], pot_ref.at[blocks], pot_sems.at[plane]),
         )
 
+    small_in_refs = (exch_in, ids_in, kinds_in, mix_in, spread_in, tz_in, ty_in)
+    small_refs = (exch_ref, ids_ref, kinds_ref, mix_ref, spread_ref, tz_ref, ty_ref)
+    small_in = [
+        pltpu.make_async_copy(source, target, small_sems.at[i])
+        for i, (source, target) in enumerate(zip(small_in_refs, small_refs))
+    ]
+    for copy in small_in:
+        copy.start()
     for plane in range(XD):
         for copy in plane_in(plane):
             copy.start()
     projector_in = pltpu.make_async_copy(proj_in_ref, proj_ref, proj_sem)
     projector_in.start()
 
+    for copy in small_in:
+        copy.wait()
+    own = ids_ref[...].astype(F32)
+    own = jnp.broadcast_to(own[0:1] * 32.0 + own[1:2], (SD, 128)).T
     row, col = iota((128, 128), 0), iota((128, 128), 1)
     halves = (row < 64) == (col < 64)
     total = jnp.zeros((SD, 128), F32)
     for source in range(ND):
         ids = exch_ref[source, 64:80, :].astype(F32)
         atoms = ids[0:1] * 32.0 + ids[1:2]
-        same = jnp.where(own_ref[...] == atoms, 1.0, 0.0).astype(BF)
+        same = jnp.where(own == atoms, 1.0, 0.0).astype(BF)
         terms = exch_ref[source, 0:64, :].astype(F32)
         terms = jnp.where(halves, jnp.concatenate([terms, terms], axis=0), 0.0).astype(BF)
         total = total + dot(same, terms)
@@ -280,7 +295,7 @@
         field_ref[block, :, :NG] = field_ref[block, :, :NG] + dot(matrix, proj_ref[s])
         return carry
 
-    lax.fori_loop(0, SD, slot, 0, unroll=8)
+    lax.fori_loop(0, SD, slot, 0, unroll=32)
 
     def plane_step(plane, carry):
         start = plane * (NG // 8)
@@ -307,23 +322,31 @@
         out_ref[:, t * 128 : t * 128 + 128] = wide_ref[t].astype(BF)
 
 
-def apply_part(tables, exchanged, own, kinds, mix, real_space, potential, projector, slot_block):
+def apply_part(tables, exchanged, ids, kinds, mix, real_space, potential, projector, slot_block):
     spread = np.zeros((128, 64), np.float32)
     for p in range(8):
         spread[p * 8 : p * 8 + 8, p::8] = 1.0
     vmem, anywhere = pl.BlockSpec(memory_space=pltpu.VMEM), pl.BlockSpec(memory_space=pl.ANY)
     return pl.pallas_call(
         apply_kernel,
-        in_specs=[pl.BlockSpec(memory_space=pltpu.SMEM)] + [vmem] * 7 + [anywhere] * 3,
+        in_specs=[pl.BlockSpec(memory_space=pltpu.SMEM)] + [anywhere] * 10,
         out_specs=vmem,
         out_shape=jax.ShapeDtypeStruct((ND * DX, LANES), BF),
         scratch_shapes=[
+            pltpu.VMEM((ND, 80, 128), BF),
+            pltpu.VMEM((16, 128), BF),
+            pltpu.VMEM((SD, 256), F32),
+            pltpu.VMEM((128, 256), F32),
+            pltpu.VMEM((128, 64), BF),
+            pltpu.VMEM((2 * KB, 512), BF),
+            pltpu.VMEM((2, NG, 256), BF),
             pltpu.VMEM((NBLK, 64, 256), BF),
             pltpu.VMEM((NBLK, 8, NG), F32),
             pltpu.VMEM((SD, 64, NG), BF),
             pltpu.VMEM((NBLK, 64, 256), F32),
             pltpu.VMEM((TILES, ND * DX, 128), F32),
             pltpu.VMEM((SD * 8, 64), F32),
+            pltpu.SemaphoreType.DMA((7,)),
             pltpu.SemaphoreType.DMA((XD,)),
             pltpu.SemaphoreType.DMA((XD,)),
             pltpu.SemaphoreType.DMA,
@@ -331,19 +354,18 @@
         compiler_params=pltpu.CompilerParams(vmem_limit_bytes=59 * MIB),
         name="apply_part",
     )(
-        slot_block, exchanged, own, kinds, mix, jnp.asarray(spread, BF),
+        slot_block, exchanged, ids, kinds, mix, jnp.asarray(spread, BF),
         tables["cz"], tables["cy"], real_space, potential, projector,
     )
 
 
-ROWS = HD * NBD
 CHUNK = 2304
 CHUNKS = KB * KB // CHUNK
 HALF = KB * KB
 
 
 def tail_kernel(
-    kz_ref, table_ref, fold0_ref, fold1_ref, rows_ref, in_ref, wave_in_ref, all_in_ref,
+    kz_ref, table_ref, in_ref, wave_in_ref, all_in_ref,
     result_ref, out_ref,
     wave_ref, all_ref, spectrum_ref, wave_sem, all_sems,
 ):
@@ -388,7 +410,7 @@
             result_ref[:, columns] = value.astype(BF)
         return carry
 
-    lax.fori_loop(0, 2 * KB // 4, flatten, 0, unroll=4)
+    lax.fori_loop(0, 2 * KB // 4, flatten, 0, unroll=8)
 
     total0, total1 = None, None
     for i in range(CHUNKS):
@@ -405,32 +427,28 @@
     total0, total1 = total0.T, total1.T
     shape = total0.shape
     keep = iota(shape, 0) % ROWS // NBD == iota(shape, 1) % ROWS // NBD
-    folded = jnp.dot(jnp.where(keep, total0, 0.0), fold0_ref[...], precision=HIGH) + jnp.dot(
-        jnp.where(keep, total1, 0.0), fold1_ref[...], precision=HIGH
-    )
-    turned = jnp.dot(folded.T[:16], rows_ref[...], precision=HIGH)
+    row, col = iota((4 * ROWS, 128), 0), iota((4 * ROWS, 128), 1)
+    place = row % NBD * 4 + row // ROWS % 2 * 2
+    d = row // (2 * ROWS)
+    fold0 = jnp.where(col == place + d, 1.0, 0.0)
+    fold1 = jnp.where(col == place + 1 - d, 2.0 * d.astype(F32) - 1.0, 0.0)
+    row, col = iota((shape[0], 128), 0), iota((shape[0], 128), 1)
+    bands = jnp.where(row // ROWS * NBD + row % NBD == col % 64, 1.0, 0.0)
+    folded = jnp.dot(jnp.where(keep, total0, 0.0), fold0, precision=HIGH) + jnp.dot(
+        jnp.where(keep, total1, 0.0), fold1, precision=HIGH
+    )
+    turned = jnp.dot(folded.T[:16], bands, precision=HIGH)
     packed = jnp.where(iota((8, 128), 1) < 64, turned[:8], turned[8:])
     for k in range(ND):
         out_ref[k] = packed
 
 
 def tail_part(table_x, first_kz, received, everything, wave):
-    fold0 = np.zeros((2, 2, HD, NBD, 128), np.float32)
-    fold1 = np.zeros((2, 2, HD, NBD, 128), np.float32)
-    for k in range(2):
-        for j in range(NBD):
-            fold0[0, k, :, j, 4 * j + 2 * k] = 1.0
-            fold0[1, k, :, j, 4 * j + 2 * k + 1] = 1.0
-            fold1[1, k, :, j, 4 * j + 2 * k] = 1.0
-            fold1[0, k, :, j, 4 * j + 2 * k + 1] = -1.0
     total = everything.shape[0]
-    row = np.arange(total)
-    band = row // ROWS * NBD + row % NBD
-    rows = (band[:, None] == np.arange(128)[None, :] % 64).astype(np.float32)
     vmem, anywhere = pl.BlockSpec(memory_space=pltpu.VMEM), pl.BlockSpec(memory_space=pl.ANY)
     return pl.pallas_call(
         tail_kernel,
-        in_specs=[pl.BlockSpec(memory_space=pltpu.SMEM)] + [vmem] * 5 + [anywhere] * 2,
+        in_specs=[pl.BlockSpec(memory_space=pltpu.SMEM)] + [vmem] * 2 + [anywhere] * 2,
         out_specs=[vmem, vmem],
         out_shape=[
             jax.ShapeDtypeStruct((ROWS, PLANE), BF),
@@ -446,8 +464,7 @@
         compiler_params=pltpu.CompilerParams(vmem_limit_bytes=50 * MIB),
         name="tail_part",
     )(
-        first_kz, table_x, jnp.asarray(fold0.reshape(-1, 128)), jnp.asarray(fold1.reshape(-1, 128)),
-        jnp.asarray(rows), received, wave, everything,
+        first_kz, table_x, received, wave, everything,
     )
 
 
@@ -468,12 +485,12 @@
     tables = {name: jnp.asarray(value) for name, value in constants().items()}
     rows = wave_coeffs.transpose(1, 0, 2)
     wave = rows.reshape(HD, NBD, 2 * KB, KB)
+
     projector = projector.reshape(SD, NPROJ, 8, NG).transpose(0, 2, 1, 3).reshape(SD, 64, NG)
     potential = local_potential.reshape(NBLK, 8, NG)
     ids = jnp.concatenate(
         [(slot_atom // 32)[None], (slot_atom % 32)[None], jnp.zeros((14, SD), jnp.int32)]
     ).astype(BF)
-    own_ids = jnp.broadcast_to(slot_atom.astype(F32)[:, None], (SD, 128))
     species = jnp.take(atom_species, slot_atom, axis=0)
     kinds = (species[:, None] == jnp.arange(256, dtype=jnp.int32)[None, :] // 64).astype(F32)
     symmetric = 0.5 * (projector_strength + jnp.swapaxes(projector_strength, 1, 2))
@@ -486,14 +503,14 @@
     sent, rows = lax.optimization_barrier((sent, rows))
     flat = rows.reshape(ROWS, PLANE)
     everything = lax.all_gather(flat, "band", axis=0, tiled=True)
-    prepared = (ids, own_ids, kinds, mix, projector, potential)
+    prepared = (ids, kinds, mix, projector, potential)
     received = exchange(sent.reshape(ND, DX, LANES)).reshape(ND * DX, LANES)
     received, prepared = lax.optimization_barrier((received, prepared))
-    ids, own_ids, kinds, mix, projector, potential = prepared
+    ids, kinds, mix, projector, potential = prepared
     terms, real_space = grid_part(tables, received, projector, slot_block, ids)
     exchanged = exchange(terms)
     sent = apply_part(
-        tables, exchanged, own_ids, kinds, mix, real_space, potential, projector, slot_block
+        tables, exchanged, ids, kinds, mix, real_space, potential, projector, slot_block
     )
     received = exchange(sent.reshape(ND, DX, LANES)).reshape(ND * DX, LANES)
     first_kz = (lax.axis_index("fft") * HD).astype(jnp.int32).reshape(1)

time: 153 us -> 145 us (0.948)
  Pallas kernels: 42.7 us -> 38 us
  local copies, waits for them, and re-layouts: 25.3 us -> 22 us
    pallas_call x1, Pallas kernels: 19.1 us -> 16.5 us  [apply_part(): pl.pallas_call(apply_kernel, in_specs=[pl.BlockSpec(memory_space=pltpu.SM...]
    unnamed x26 -> x20, local copies, waits for them, and re-layouts: 8.86 us -> 6.35 us
    pallas_call x1, Pallas kernels: 11.5 us -> 9.39 us  [grid_part(): pl.pallas_call(grid_kernel, in_specs=[pl.BlockSpec(memory_space=pltpu.SME...]
  transfers between devices with their start and end apart: 4 -> 4, of which waited for: 3 -> 3; matrix products, arithmetic and copies ran while one was open for 12% -> 12% of each run, Pallas kernels for 20% -> 18%
where the time goes in v3:
time: 145 us
  waiting for transfers between devices  41 us (28%)
  Pallas kernels  38 us (26%)
  local copies, waits for them, and re-layouts  22 us (15%)
  starting transfers between devices  14.5 us (10%)
  between operations  14.2 us (10%)
  blocking collectives  13.3 us (9%)
  other arithmetic  1.85 us (1%)
    all_to_all x3, waiting for transfers between devices, exchange(): return lax.all_to_all(array, 'fft', split_axis=0, concat_axis=0, tiled=True)  41 us
    pallas_call x1, Pallas kernels, apply_part(): pl.pallas_call(apply_kernel, in_specs=[pl.BlockSpec(memory_space=pltpu.SM...  16.5 us
    all_to_all x3, starting transfers between devices, exchange(): return lax.all_to_all(array, 'fft', split_axis=0, concat_axis=0, tiled=True)  14.4 us
    all_to_all x1, blocking collectives, exchange(): return lax.all_to_all(array, 'fft', split_axis=0, concat_axis=0, tiled=True)  13.3 us
    pallas_call x1, Pallas kernels, tail_part(): pl.pallas_call(tail_kernel, in_specs=[pl.BlockSpec(memory_space=pltpu.SME...  9.99 us
    pallas_call x1, Pallas kernels, grid_part(): pl.pallas_call(grid_kernel, in_specs=[pl.BlockSpec(memory_space=pltpu.SME...  9.39 us
    unnamed x20, local copies, waits for them, and re-layouts  6.35 us
    transpose x1, local copies, waits for them, and re-layouts, on_device(): projector.reshape(SD, NPROJ, 8, NG).transpose(0, 2, 1, 3)  4.82 us
  transfers between devices with their start and end apart: 4, of which 3 were waited for; matrix products, arithmetic and copies ran while one was open for 12% of the time, Pallas kernels for 18%

profile of v3, /device:TPU:160, one launch (start us, length us, event | category | flops | bytes accessed | tf_op | source)
XLA Modules:
  0.0 144.8 jit_solution(14004902593725908911)
XLA Ops:
  7.2 2.1 %reshape.140.wave_ref = bf16[6,4,192,96]{3,2,1,0:T(8,128)(2,1)S(1)} reshape(bf16[6,4,18432]{2,1,0:T(4,128)(2,1)} %bitcast.34) | data formatting | bytes 1769472 | tf_op jit(solution)/shard_map/reshape | solution.py:487
  9.4 0.9 copy-done.2
  10.3 2.1 %x_transform.1 = bf16[384,2304]{1,0:T(8,128)(2,1)} custom-call(bf16[384,192]{1,0:T(8,128)(2,1)S(1)} %copy-done.2, bf16[6,4,192,96]{3,2,1,0:T(8,128)(2,1)S(1)} %reshape.140.wave_ref), custom_call_target="tpu_custom_call" | custom-call | tf_op jit(solution)/shard_map/x_transform/pallas_call | solution.py:90
  12.4 1.1 reshape.148.wave_in_ref
  13.5 7.1 %all-to-all-start = ((bf16[16,24,2304]{2,1,0:T(8,128)(2,1)}), bf16[16,24,2304]{2,1,0:T(8,128)(2,1)}, u32[]{:S(2)}, u32[]{:S(2)}) async-start(bf16[16,24,2304]{2,1,0:T(8,128)(2,1)} %bitcast.2), calls=%async_computation | async-start | bytes 3538944 | tf_op jit(solution)/shard_map/all_to_all | solution.py:472
  20.6 3.8 %copy.27 = bf16[128,8,1536]{0,2,1:T(8,128)(2,1)S(1)} copy(bf16[128,8,1536]{2,1,0:T(8,128)(2,1)} %param.18) | data formatting | bytes 6291456 | tf_op args[2]
  24.4 4.8 %copy.28 = bf16[128,8,8,192]{3,2,1,0:T(8,128)(2,1)} copy(bf16[128,8,8,192]{0,3,1,2:T(8,128)(2,1)S(1)} %bitcast.32) | data formatting | bytes 6291456 | tf_op jit(solution)/shard_map/transpose | solution.py:489
  29.2 3.4 %reshape.145.pot_in_ref = f32[288,8,192]{2,1,0:T(8,128)} reshape(f32[12,36864]{1,0:T(8,128)} %param.17) | data formatting | bytes 3538944 | tf_op jit(solution)/shard_map/reshape | solution.py:490
  33.8 1.0 gather_fusion
  34.9 0.7 pad.4.mix_in
  35.6 0.7 maximum_maximum_fusion.ids_ref.ids_in
  36.2 0.7 compare_convert_fusion.kinds_in
  36.9 10.7 %all-to-all-done = bf16[16,24,2304]{2,1,0:T(8,128)(2,1)} async-done(((bf16[16,24,2304]{2,1,0:T(8,128)(2,1)}), bf16[16,24,2304]{2,1,0:T(8,128)(2,1)}, u32[]{:S(2)}, u32[]{:S(2)}) %all-to-all-start) | async-done | bytes 1769504 | tf_op jit(solution)/shard_map/all_to_all | solution.py:472
  47.6 9.4 %grid_part.1 = (bf16[16,80,128]{2,1,0:T(8,128)(2,1)}, bf16[288,64,256]{2,1,0:T(8,128)(2,1)}) custom-call(s32[128]{0:T(128)} %slot_ref.3, bf16[192,256]{1,0:T(8,128)(2,1)} %constant.92.clone.ty_ref, bf16[192,512]{1,0:T(8,128)(2,1)} %constant.93.clone.tz_ref, bf16[64,128]{1,0:T(8,128)(2,1)} %constant.97.clone.fold_ref, ...), custom_call_target="tpu_custom_call" | custom-call | tf_op jit(solution)/shard_map/grid_part/pallas_call | solution.py:198
  57.0 13.3 %all_to_all.20.exch_in = bf16[16,80,128]{2,1,0:T(8,128)(2,1)} all-to-all(bf16[16,80,128]{2,1,0:T(8,128)(2,1)} %get-tuple-element.18), channel_id=1, replica_groups=mesh['band'=16,'fft'=16] {'fft'}, dimensions={0} | all-to-all | bytes 655360 | tf_op jit(solution)/shard_map/all_to_all | solution.py:472
  70.3 16.5 %apply_part.1 = bf16[384,2304]{1,0:T(8,128)(2,1)} custom-call(s32[128]{0:T(128)} %slot_ref.3, bf16[16,80,128]{2,1,0:T(8,128)(2,1)} %all_to_all.20.exch_in, bf16[16,128]{1,0:T(8,128)(2,1)} %maximum_maximum_fusion.ids_ref.ids_in, f32[128,256]{1,0:T(8,128)} %compare_convert_fusion.kinds_in, f32[128,256]{1,0:T(8,128)} %pad.4.mix_in, ...), custom_call_target="tpu_custom_call" | custom-call | tf_op jit(solution)/shard_map/apply_part/pallas_call | solution.py:330
  86.9 3.9 %all-to-all-start.2 = ((bf16[16,24,2304]{2,1,0:T(8,128)(2,1)}), bf16[16,24,2304]{2,1,0:T(8,128)(2,1)S(1)}, u32[]{:S(2)}, u32[]{:S(2)}) async-start(bf16[16,24,2304]{2,1,0:T(8,128)(2,1)} %bitcast.33), calls=%async_computation.2 | async-start | bytes 3538944 | tf_op jit(solution)/shard_map/all_to_all | solution.py:472
  90.7 23.9 %all-to-all-done.2 = bf16[16,24,2304]{2,1,0:T(8,128)(2,1)S(1)} async-done(((bf16[16,24,2304]{2,1,0:T(8,128)(2,1)}), bf16[16,24,2304]{2,1,0:T(8,128)(2,1)S(1)}, u32[]{:S(2)}, u32[]{:S(2)}) %all-to-all-start.2) | async-done | bytes 1769504 | tf_op jit(solution)/shard_map/all_to_all | solution.py:472
  114.6 0.9 copy-done.3
  115.5 10.0 %tail_part.1 = (bf16[24,18432]{1,0:T(8,128)(2,1)S(1)}, f32[16,8,128]{2,1,0:T(8,128)S(1)}) custom-call(s32[1]{0:T(128)} %bitcast.kz_ref, bf16[192,384]{1,0:T(8,128)(2,1)S(1)} %copy-done.3, bf16[384,2304]{1,0:T(8,128)(2,1)S(1)} %bitcast.29, bf16[24,18432]{1,0:T(8,128)(2,1)S(1)} %copy-done.1, bf16[384,18432]{1,0:T(8,128)(2,1)} %all-gather.2.cloned.1.call-done.all_in_ref), custom_call_target="tpu_custom_call" | custom-call | tf_op jit(solution)/shard_map/tail_part/pallas_call | solution.py:449
  125.5 0.6 copy-done.4
  126.2 3.5 %all-to-all-start.3 = ((f32[16,8,128]{2,1,0:T(8,128)}), f32[16,8,128]{2,1,0:T(8,128)S(1)}, u32[]{:S(2)}, u32[]{:S(2)}) async-start(f32[16,8,128]{2,1,0:T(8,128)} %copy-done.4), calls=%async_computation.3 | async-start | bytes 131072 | tf_op jit(solution)/shard_map/all_to_all | solution.py:472
  129.7 1.2 reshape.149
  130.9 6.4 %all-to-all-done.3 = f32[16,8,128]{2,1,0:T(8,128)S(1)} async-done(((f32[16,8,128]{2,1,0:T(8,128)}), f32[16,8,128]{2,1,0:T(8,128)S(1)}, u32[]{:S(2)}, u32[]{:S(2)}) %all-to-all-start.3) | async-done | bytes 65568 | tf_op jit(solution)/shard_map/all_to_all | solution.py:472
  (36 shorter events, 2.0 us)
Async XLA Ops:
  7.2 26.6 %copy-start = (s32[1000]{0:T(1024)S(1)}, s32[1000]{0:T(1024)}, u32[]{:S(2)}) copy-start(s32[1000]{0:T(1024)} %param.21) | copy-start | bytes 12004
  7.2 107.4 %all-gather.2.cloned.1.call-start = ((), (), s32[]{:S(2)}) async-start(), calls=%async_computation.4 | async-start | bytes 15040512 | tf_op jit(solution)/shard_map/all_gather | solution.py:505
  7.2 5.1 %copy-start.5 = (bf16[4,6,18432]{2,0,1:T(4,128)(2,1)S(1)}, bf16[4,6,18432]{2,0,1:T(4,128)(2,1)}, u32[]{:S(2)}) copy-start(bf16[4,6,18432]{2,0,1:T(4,128)(2,1)} %param.16) | copy-start | bytes 2654212
  9.3 0.9 copy-start.2
  13.5 34.1 %all-to-all-start = ((bf16[16,24,2304]{2,1,0:T(8,128)(2,1)}), bf16[16,24,2304]{2,1,0:T(8,128)(2,1)}, u32[]{:S(2)}, u32[]{:S(2)}) async-start(bf16[16,24,2304]{2,1,0:T(8,128)(2,1)} %bitcast.2), calls=%async_computation | async-start | bytes 3538944 | tf_op jit(solution)/shard_map/all_to_all | solution.py:472
  29.2 3.4 %copy-start.6 = (f32[4,8,8]{2,1,0:T(8,128)S(1)}, f32[4,8,8]{2,1,0:T(8,128)}, u32[]{:S(2)}) copy-start(f32[4,8,8]{2,1,0:T(8,128)} %param.23) | copy-start | bytes 3076
  29.2 3.5 %copy-start.7 = (s32[4]{0:T(128)S(1)}, s32[4]{0:T(128)}, u32[]{:S(2)}) copy-start(s32[4]{0:T(128)} %param.22) | copy-start | bytes 52
  29.2 4.5 %copy-start.8 = (s32[128]{0:T(128)S(1)}, s32[128]{0:T(128)}, u32[]{:S(2)}) copy-start(s32[128]{0:T(128)} %param.20) | copy-start | bytes 1540
  86.8 27.8 %copy-start.1 = (bf16[24,18432]{1,0:T(8,128)(2,1)S(1)}, bf16[24,18432]{1,0:T(8,128)(2,1)}, u32[]{:S(2)}) copy-start(bf16[24,18432]{1,0:T(8,128)(2,1)} %reshape.148.wave_in_ref) | copy-start | bytes 2654212
  86.9 27.8 %all-to-all-start.2 = ((bf16[16,24,2304]{2,1,0:T(8,128)(2,1)}), bf16[16,24,2304]{2,1,0:T(8,128)(2,1)S(1)}, u32[]{:S(2)}, u32[]{:S(2)}) async-start(bf16[16,24,2304]{2,1,0:T(8,128)(2,1)} %bitcast.33), calls=%async_computation.2 | async-start | bytes 3538944 | tf_op jit(solution)/shard_map/all_to_all | solution.py:472
  114.6 0.9 copy-start.3
  125.5 0.6 copy-start.4
  126.2 11.1 %all-to-all-start.3 = ((f32[16,8,128]{2,1,0:T(8,128)}), f32[16,8,128]{2,1,0:T(8,128)S(1)}, u32[]{:S(2)}, u32[]{:S(2)}) async-start(f32[16,8,128]{2,1,0:T(8,128)} %copy-done.4), calls=%async_computation.3 | async-start | bytes 131072 | tf_op jit(solution)/shard_map/all_to_all | solution.py:472
Sparse Core Ops, SparseCore 0:
  13.6 82.2 all-gather.1

commit v4 on v3

--- a/solution.py
+++ b/solution.py
@@ -224,8 +224,8 @@
     real_in_ref, pot_in_ref, proj_in_ref,
     out_ref,
     exch_ref, ids_ref, kinds_ref, mix_ref, spread_ref, tz_ref, ty_ref,
-    real_ref, pot_ref, proj_ref, field_ref, wide_ref, weight_ref,
-    small_sems, real_sems, pot_sems, proj_sem,
+    real_ref, pot_ref, proj_ref, field_ref, wide_ref, weight_ref, sent_ref,
+    small_sems, real_sems, pot_sems, proj_sem, out_sems,
 ):
     def plane_in(plane):
         blocks = pl.ds(plane * (NG // 8), NG // 8)
@@ -295,7 +295,7 @@
         field_ref[block, :, :NG] = field_ref[block, :, :NG] + dot(matrix, proj_ref[s])
         return carry
 
-    lax.fori_loop(0, SD, slot, 0, unroll=32)
+    lax.fori_loop(0, SD, slot, 0, unroll=64)
 
     def plane_step(plane, carry):
         start = plane * (NG // 8)
@@ -317,20 +317,28 @@
                     wide_ref[3 * h + v, rows, :] = joined[v][16 * h : 16 * h + 16]
         return carry
 
-    lax.fori_loop(0, XD, plane_step, 0, unroll=PLANE_UNROLL)
-    for t in range(TILES):
-        out_ref[:, t * 128 : t * 128 + 128] = wide_ref[t].astype(BF)
+    lax.fori_loop(0, XD, plane_step, 0, unroll=XD)
+    def columns_out(h):
+        columns = pl.ds(h * GROUP, GROUP)
+        return pltpu.make_async_copy(sent_ref.at[:, columns], out_ref.at[:, columns], out_sems.at[h])
+
+    for h in range(HD):
+        for t in range(3 * h, 3 * h + 3):
+            sent_ref[:, t * 128 : t * 128 + 128] = wide_ref[t].astype(BF)
+        columns_out(h).start()
+    for h in range(HD):
+        columns_out(h).wait()
 
 
 def apply_part(tables, exchanged, ids, kinds, mix, real_space, potential, projector, slot_block):
     spread = np.zeros((128, 64), np.float32)
     for p in range(8):
         spread[p * 8 : p * 8 + 8, p::8] = 1.0
-    vmem, anywhere = pl.BlockSpec(memory_space=pltpu.VMEM), pl.BlockSpec(memory_space=pl.ANY)
+    anywhere = pl.BlockSpec(memory_space=pl.ANY)
     return pl.pallas_call(
         apply_kernel,
         in_specs=[pl.BlockSpec(memory_space=pltpu.SMEM)] + [anywhere] * 10,
-        out_specs=vmem,
+        out_specs=anywhere,
         out_shape=jax.ShapeDtypeStruct((ND * DX, LANES), BF),
         scratch_shapes=[
             pltpu.VMEM((ND, 80, 128), BF),
@@ -346,10 +354,12 @@
             pltpu.VMEM((NBLK, 64, 256), F32),
             pltpu.VMEM((TILES, ND * DX, 128), F32),
             pltpu.VMEM((SD * 8, 64), F32),
+            pltpu.VMEM((ND * DX, LANES), BF),
             pltpu.SemaphoreType.DMA((7,)),
             pltpu.SemaphoreType.DMA((XD,)),
             pltpu.SemaphoreType.DMA((XD,)),
             pltpu.SemaphoreType.DMA,
+            pltpu.SemaphoreType.DMA((HD,)),
         ],
         compiler_params=pltpu.CompilerParams(vmem_limit_bytes=59 * MIB),
         name="apply_part",

time: 145 us -> 145 us (level)
  transfers between devices with their start and end apart: 4 -> 4, of which waited for: 3 -> 3; matrix products, arithmetic and copies ran while one was open for 12% -> 12% of each run, Pallas kernels for 18% -> 17%
where the time goes in v4:
time: 145 us; the launch traced here: 144 us
  waiting for transfers between devices  41 us (28%)
  Pallas kernels  37.2 us (26%)
  local copies, waits for them, and re-layouts  22 us (15%)
  starting transfers between devices  14.5 us (10%)
  between operations  14.2 us (10%)
  blocking collectives  13.3 us (9%)
  other arithmetic  1.85 us (1%)
    all_to_all x3, waiting for transfers between devices, exchange(): return lax.all_to_all(array, 'fft', split_axis=0, concat_axis=0, tiled=True)  41 us
    pallas_call x1, Pallas kernels, apply_part(): pl.pallas_call(apply_kernel, in_specs=[pl.BlockSpec(memory_space=pltpu.SM...  15.7 us
    all_to_all x3, starting transfers between devices, exchange(): return lax.all_to_all(array, 'fft', split_axis=0, concat_axis=0, tiled=True)  14.4 us
    all_to_all x1, blocking collectives, exchange(): return lax.all_to_all(array, 'fft', split_axis=0, concat_axis=0, tiled=True)  13.3 us
    pallas_call x1, Pallas kernels, tail_part(): pl.pallas_call(tail_kernel, in_specs=[pl.BlockSpec(memory_space=pltpu.SME...  9.99 us
    pallas_call x1, Pallas kernels, grid_part(): pl.pallas_call(grid_kernel, in_specs=[pl.BlockSpec(memory_space=pltpu.SME...  9.39 us
    unnamed x20, local copies, waits for them, and re-layouts  6.35 us
    transpose x1, local copies, waits for them, and re-layouts, on_device(): projector.reshape(SD, NPROJ, 8, NG).transpose(0, 2, 1, 3)  4.82 us
  transfers between devices with their start and end apart: 4, of which 3 were waited for; matrix products, arithmetic and copies ran while one was open for 12% of the time, Pallas kernels for 17%

profile of v4, /device:TPU:160, one launch (start us, length us, event | category | flops | bytes accessed | tf_op | source)
XLA Modules:
  0.0 144.0 jit_solution(12575755861413990406)
XLA Ops:
  7.2 2.1 %reshape.140.wave_ref = bf16[6,4,192,96]{3,2,1,0:T(8,128)(2,1)S(1)} reshape(bf16[6,4,18432]{2,1,0:T(4,128)(2,1)} %bitcast.34) | data formatting | bytes 1769472 | tf_op jit(solution)/shard_map/reshape | solution.py:497
  9.4 0.9 copy-done.2
  10.3 2.1 %x_transform.1 = bf16[384,2304]{1,0:T(8,128)(2,1)} custom-call(bf16[384,192]{1,0:T(8,128)(2,1)S(1)} %copy-done.2, bf16[6,4,192,96]{3,2,1,0:T(8,128)(2,1)S(1)} %reshape.140.wave_ref), custom_call_target="tpu_custom_call" | custom-call | tf_op jit(solution)/shard_map/x_transform/pallas_call | solution.py:90
  12.4 1.1 reshape.148.wave_in_ref
  13.5 7.1 %all-to-all-start = ((bf16[16,24,2304]{2,1,0:T(8,128)(2,1)}), bf16[16,24,2304]{2,1,0:T(8,128)(2,1)}, u32[]{:S(2)}, u32[]{:S(2)}) async-start(bf16[16,24,2304]{2,1,0:T(8,128)(2,1)} %bitcast.2), calls=%async_computation | async-start | bytes 3538944 | tf_op jit(solution)/shard_map/all_to_all | solution.py:482
  20.6 3.8 %copy.27 = bf16[128,8,1536]{0,2,1:T(8,128)(2,1)S(1)} copy(bf16[128,8,1536]{2,1,0:T(8,128)(2,1)} %param.18) | data formatting | bytes 6291456 | tf_op args[2]
  24.4 4.8 %copy.28 = bf16[128,8,8,192]{3,2,1,0:T(8,128)(2,1)} copy(bf16[128,8,8,192]{0,3,1,2:T(8,128)(2,1)S(1)} %bitcast.32) | data formatting | bytes 6291456 | tf_op jit(solution)/shard_map/transpose | solution.py:499
  29.2 3.4 %reshape.145.pot_in_ref = f32[288,8,192]{2,1,0:T(8,128)} reshape(f32[12,36864]{1,0:T(8,128)} %param.17) | data formatting | bytes 3538944 | tf_op jit(solution)/shard_map/reshape | solution.py:500
  33.8 1.0 gather_fusion
  34.9 0.7 pad.4.mix_in
  35.6 0.7 maximum_maximum_fusion.ids_ref.ids_in
  36.2 0.7 compare_convert_fusion.kinds_in
  36.9 10.7 %all-to-all-done = bf16[16,24,2304]{2,1,0:T(8,128)(2,1)} async-done(((bf16[16,24,2304]{2,1,0:T(8,128)(2,1)}), bf16[16,24,2304]{2,1,0:T(8,128)(2,1)}, u32[]{:S(2)}, u32[]{:S(2)}) %all-to-all-start) | async-done | bytes 1769504 | tf_op jit(solution)/shard_map/all_to_all | solution.py:482
  47.6 9.4 %grid_part.1 = (bf16[16,80,128]{2,1,0:T(8,128)(2,1)}, bf16[288,64,256]{2,1,0:T(8,128)(2,1)}) custom-call(s32[128]{0:T(128)} %slot_ref.3, bf16[192,256]{1,0:T(8,128)(2,1)} %constant.92.clone.ty_ref, bf16[192,512]{1,0:T(8,128)(2,1)} %constant.93.clone.tz_ref, bf16[64,128]{1,0:T(8,128)(2,1)} %constant.97.clone.fold_ref, ...), custom_call_target="tpu_custom_call" | custom-call | tf_op jit(solution)/shard_map/grid_part/pallas_call | solution.py:198
  57.0 13.3 %all_to_all.20.exch_in = bf16[16,80,128]{2,1,0:T(8,128)(2,1)} all-to-all(bf16[16,80,128]{2,1,0:T(8,128)(2,1)} %get-tuple-element.18), channel_id=1, replica_groups=mesh['band'=16,'fft'=16] {'fft'}, dimensions={0} | all-to-all | bytes 655360 | tf_op jit(solution)/shard_map/all_to_all | solution.py:482
  70.3 15.7 %apply_part.1 = bf16[384,2304]{1,0:T(8,128)(2,1)} custom-call(s32[128]{0:T(128)} %slot_ref.3, bf16[16,80,128]{2,1,0:T(8,128)(2,1)} %all_to_all.20.exch_in, bf16[16,128]{1,0:T(8,128)(2,1)} %maximum_maximum_fusion.ids_ref.ids_in, f32[128,256]{1,0:T(8,128)} %compare_convert_fusion.kinds_in, f32[128,256]{1,0:T(8,128)} %pad.4.mix_in, ...), custom_call_target="tpu_custom_call" | custom-call | tf_op jit(solution)/shard_map/apply_part/pallas_call | solution.py:338
  86.0 3.9 %all-to-all-start.2 = ((bf16[16,24,2304]{2,1,0:T(8,128)(2,1)}), bf16[16,24,2304]{2,1,0:T(8,128)(2,1)S(1)}, u32[]{:S(2)}, u32[]{:S(2)}) async-start(bf16[16,24,2304]{2,1,0:T(8,128)(2,1)} %bitcast.33), calls=%async_computation.2 | async-start | bytes 3538944 | tf_op jit(solution)/shard_map/all_to_all | solution.py:482
  89.9 23.9 %all-to-all-done.2 = bf16[16,24,2304]{2,1,0:T(8,128)(2,1)S(1)} async-done(((bf16[16,24,2304]{2,1,0:T(8,128)(2,1)}), bf16[16,24,2304]{2,1,0:T(8,128)(2,1)S(1)}, u32[]{:S(2)}, u32[]{:S(2)}) %all-to-all-start.2) | async-done | bytes 1769504 | tf_op jit(solution)/shard_map/all_to_all | solution.py:482
  113.8 0.9 copy-done.3
  114.7 10.0 %tail_part.1 = (bf16[24,18432]{1,0:T(8,128)(2,1)S(1)}, f32[16,8,128]{2,1,0:T(8,128)S(1)}) custom-call(s32[1]{0:T(128)} %bitcast.kz_ref, bf16[192,384]{1,0:T(8,128)(2,1)S(1)} %copy-done.3, bf16[384,2304]{1,0:T(8,128)(2,1)S(1)} %bitcast.29, bf16[24,18432]{1,0:T(8,128)(2,1)S(1)} %copy-done.1, bf16[384,18432]{1,0:T(8,128)(2,1)} %all-gather.2.cloned.1.call-done.all_in_ref), custom_call_target="tpu_custom_call" | custom-call | tf_op jit(solution)/shard_map/tail_part/pallas_call | solution.py:459
  124.7 0.6 copy-done.4
  125.3 3.5 %all-to-all-start.3 = ((f32[16,8,128]{2,1,0:T(8,128)}), f32[16,8,128]{2,1,0:T(8,128)S(1)}, u32[]{:S(2)}, u32[]{:S(2)}) async-start(f32[16,8,128]{2,1,0:T(8,128)} %copy-done.4), calls=%async_computation.3 | async-start | bytes 131072 | tf_op jit(solution)/shard_map/all_to_all | solution.py:482
  128.8 1.2 reshape.149
  130.1 6.4 %all-to-all-done.3 = f32[16,8,128]{2,1,0:T(8,128)S(1)} async-done(((f32[16,8,128]{2,1,0:T(8,128)}), f32[16,8,128]{2,1,0:T(8,128)S(1)}, u32[]{:S(2)}, u32[]{:S(2)}) %all-to-all-start.3) | async-done | bytes 65568 | tf_op jit(solution)/shard_map/all_to_all | solution.py:482
  (36 shorter events, 2.0 us)
Async XLA Ops:
  7.2 26.6 %copy-start = (s32[1000]{0:T(1024)S(1)}, s32[1000]{0:T(1024)}, u32[]{:S(2)}) copy-start(s32[1000]{0:T(1024)} %param.21) | copy-start | bytes 12004
  7.2 106.6 %all-gather.2.cloned.1.call-start = ((), (), s32[]{:S(2)}) async-start(), calls=%async_computation.4 | async-start | bytes 15040512 | tf_op jit(solution)/shard_map/all_gather | solution.py:515
  7.2 5.1 %copy-start.5 = (bf16[4,6,18432]{2,0,1:T(4,128)(2,1)S(1)}, bf16[4,6,18432]{2,0,1:T(4,128)(2,1)}, u32[]{:S(2)}) copy-start(bf16[4,6,18432]{2,0,1:T(4,128)(2,1)} %param.16) | copy-start | bytes 2654212
  9.3 0.9 copy-start.2
  13.5 34.1 %all-to-all-start = ((bf16[16,24,2304]{2,1,0:T(8,128)(2,1)}), bf16[16,24,2304]{2,1,0:T(8,128)(2,1)}, u32[]{:S(2)}, u32[]{:S(2)}) async-start(bf16[16,24,2304]{2,1,0:T(8,128)(2,1)} %bitcast.2), calls=%async_computation | async-start | bytes 3538944 | tf_op jit(solution)/shard_map/all_to_all | solution.py:482
  29.2 3.4 %copy-start.6 = (f32[4,8,8]{2,1,0:T(8,128)S(1)}, f32[4,8,8]{2,1,0:T(8,128)}, u32[]{:S(2)}) copy-start(f32[4,8,8]{2,1,0:T(8,128)} %param.23) | copy-start | bytes 3076
  29.2 3.5 %copy-start.7 = (s32[4]{0:T(128)S(1)}, s32[4]{0:T(128)}, u32[]{:S(2)}) copy-start(s32[4]{0:T(128)} %param.22) | copy-start | bytes 52
  29.2 4.5 %copy-start.8 = (s32[128]{0:T(128)S(1)}, s32[128]{0:T(128)}, u32[]{:S(2)}) copy-start(s32[128]{0:T(128)} %param.20) | copy-start | bytes 1540
  86.0 27.8 %copy-start.1 = (bf16[24,18432]{1,0:T(8,128)(2,1)S(1)}, bf16[24,18432]{1,0:T(8,128)(2,1)}, u32[]{:S(2)}) copy-start(bf16[24,18432]{1,0:T(8,128)(2,1)} %reshape.148.wave_in_ref) | copy-start | bytes 2654212
  86.0 27.8 %all-to-all-start.2 = ((bf16[16,24,2304]{2,1,0:T(8,128)(2,1)}), bf16[16,24,2304]{2,1,0:T(8,128)(2,1)S(1)}, u32[]{:S(2)}, u32[]{:S(2)}) async-start(bf16[16,24,2304]{2,1,0:T(8,128)(2,1)} %bitcast.33), calls=%async_computation.2 | async-start | bytes 3538944 | tf_op jit(solution)/shard_map/all_to_all | solution.py:482
  113.8 0.9 copy-start.3
  124.7 0.6 copy-start.4
  125.3 11.1 %all-to-all-start.3 = ((f32[16,8,128]{2,1,0:T(8,128)}), f32[16,8,128]{2,1,0:T(8,128)S(1)}, u32[]{:S(2)}, u32[]{:S(2)}) async-start(f32[16,8,128]{2,1,0:T(8,128)} %copy-done.4), calls=%async_computation.3 | async-start | bytes 131072 | tf_op jit(solution)/shard_map/all_to_all | solution.py:482
Sparse Core Ops, SparseCore 0:
  13.6 82.2 all-gather.1
